TPU v7x, 256 devices: a whole 4x4x8 slice. The times are simulated.
256 devices in a mesh: row: 16 (over x_hi, z), col: 16 (over y, x_lo, core).
Axes of the slice: x: 4 (x_hi: 2, x_lo: 2; x = x_hi * 2 + x_lo), y: 4, z: 8, core: 2. Of those that a mesh axis runs over, the one named last changes fastest.
Arguments:
- panel: bfloat16 [1536, 147456], P('col', 'row'), may hold values from -3 to 3
- eigenvalues: float32 [1536], P('col'), may hold values from 0.3 to 3
- positions: float32 [3, 49152], P(None, 'row'), may hold values from -6 to 6
- elements: int32 [49152], P('row'), may hold values from 0 to 4
- radii: float32 [5], replicated, may hold values from 0.5 to 2
- neighbors: int32 [384, 5], P('row'), may hold values from 0 to 383, as said below
Outputs:
- forces: float32 [3, 49152], P(None, ('row', 'col'))
Inputs may be any that keep to these rules, and one draw needn't show every extreme that they name: neighbors[I, k] lies within 24 tiles of I; slot 0 holds I + 24 and slot 1 holds I - 24, each clamped to the tiles that exist; the others are distinct offsets within that reach, clamped.
All inputs are finite; a program needn't handle non-finite values.
Results may differ from a plain program's by a relative error of at most 0.0029.
Values may be sent and summed in bfloat16 or wider, within the bound.
No kernel may reach another device: no remote copies, remote signals or barrier semaphores. Data moves between devices by JAX's collectives and lax.ppermute only.
A program may use at most 64 MiB of HBM per device.

v0:
```python
import jax
import jax.numpy as jnp
from jax import lax
from jax.sharding import PartitionSpec as P

BLK = 128


def extended(cells, sides, width):
    for axis, dim in sides:
        count = lax.axis_size(axis)
        ends = count - 1
        head = lax.slice_in_dim(cells, 0, width, axis=dim)
        tail = lax.slice_in_dim(cells, cells.shape[dim] - width, cells.shape[dim], axis=dim)
        cells = jnp.concatenate(
            [
                lax.ppermute(tail, axis, [(i, (i + 1) % count) for i in range(ends)]),
                cells,
                lax.ppermute(head, axis, [((i + 1) % count, i) for i in range(ends)]),
            ],
            axis=dim,
        )
    return cells


def atom_radius(elements, radii):
    table = (elements[None, :] == jnp.arange(radii.shape[0], dtype=jnp.int32)[:, None]).astype(
        jnp.float32
    )
    return jnp.sum(table * radii[:, None], axis=0)


def pair_forces(left, right, geo_i, geo_j, tile_size):
    coupling = lax.dot_general(
        left, right, (((0,), (0,)), ((), ())), preferred_element_type=jnp.float32
    )
    coupling = coupling.reshape(3, tile_size, 3, tile_size)
    delta = geo_i[:3, :, None] - geo_j[:3, None, :]
    spread = geo_i[3][:, None] + geo_j[3][None, :]
    inverse = 1.0 / (jnp.sum(delta * delta, axis=0) + spread * spread)
    fifth = inverse * inverse * jnp.sqrt(inverse)
    seventh = fifth * inverse
    trace = coupling[0, :, 0, :] + coupling[1, :, 1, :] + coupling[2, :, 2, :]
    along = []
    across = []
    for comp in range(3):
        along.append(
            coupling[comp, :, 0, :] * delta[0]
            + coupling[comp, :, 1, :] * delta[1]
            + coupling[comp, :, 2, :] * delta[2]
        )
        across.append(
            coupling[0, :, comp, :] * delta[0]
            + coupling[1, :, comp, :] * delta[1]
            + coupling[2, :, comp, :] * delta[2]
        )
    quad = delta[0] * along[0] + delta[1] * along[1] + delta[2] * along[2]
    rows = []
    for comp in range(3):
        term = (
            3.0 * fifth * (trace * delta[comp] + along[comp] + across[comp])
            - 15.0 * seventh * quad * delta[comp]
        )
        rows.append(-jnp.sum(term, axis=1))
    return jnp.stack(rows, axis=0)


def tile_forces(scaled_own, panel_ext, geo_own, geo_ext, nbr_rows, base_tile, tile_size):
    width = 3 * tile_size
    slots = nbr_rows.shape[1]

    def one_tile(index):
        left = lax.dynamic_slice_in_dim(scaled_own, index * width, width, 1)
        geo_i = lax.dynamic_slice_in_dim(geo_own, index * tile_size, tile_size, 1)
        total = jnp.zeros((3, tile_size), jnp.float32)
        for slot in range(slots):
            local = nbr_rows[index, slot] - base_tile
            right = lax.dynamic_slice_in_dim(panel_ext, local * width, width, 1)
            geo_j = lax.dynamic_slice_in_dim(geo_ext, local * tile_size, tile_size, 1)
            total = total + pair_forces(left, right, geo_i, geo_j, tile_size)
        return total

    count_tiles = scaled_own.shape[1] // width
    result = lax.map(one_tile, jnp.arange(count_tiles, dtype=jnp.int32))
    return jnp.transpose(result, (1, 0, 2)).reshape(3, -1)


def per_device(panel, eigenvalues, positions, elements, radii, neighbors):
    weights = 0.25 / jnp.sqrt(eigenvalues)
    scaled = (panel.astype(jnp.float32) * weights[:, None]).astype(jnp.bfloat16)
    geometry = jnp.concatenate([positions, atom_radius(elements, radii)[None, :]], axis=0)
    own_atoms = positions.shape[1]
    tiles_own = own_atoms // BLK
    first_tile = lax.axis_index("row") * tiles_own
    panel_ext = extended(panel, (("row", 1),), 3 * own_atoms)
    geo_ext = extended(geometry, (("row", 1),), own_atoms)
    base_tile = first_tile - tiles_own
    partial_forces = tile_forces(scaled, panel_ext, geometry, geo_ext, neighbors, base_tile, BLK)
    result = lax.psum_scatter(partial_forces, "col", scatter_dimension=1, tiled=True)
    return result


def solution(mesh):
    return jax.shard_map(
        per_device,
        mesh=mesh,
        in_specs=(P("col", "row"), P("col"), P(None, "row"), P("row"), P(), P("row", None)),
        out_specs=P(None, ("row", "col")),
        check_vma=False,
    )
```

profile of v0, /device:TPU:4, one launch (start us, length us, event | category | flops | bytes accessed | tf_op | source)
XLA Modules:
  0.0 620.0 jit_solution(11750926704915157389)
XLA Ops:
  8.3 3.8 collective-permute-start
  12.2 5.8 collective-permute-start.1
  18.0 1.9 collective-permute-start.2
  19.9 7.5 %collective-permute-start.3 = (bf16[96,9216]{1,0:T(8,128)(2,1)}, bf16[96,9216]{1,0:T(8,128)(2,1)}, u32[]{:S(2)}, u32[]{:S(2)}) collective-permute-start(bf16[96,9216]{1,0:T(8,128)(2,1)} %param.8), channel_id=1, source_target_pairs={{16,0},{32,16},{48,32},{64,48},{80,64},{96,80},{112,96},{128,112},... | collective-permute-start | bytes 5308424 | tf_op jit(solution)/shard_map/ppermute | solution.py:19
  28.1 3.1 multiply_convert_fusion
  31.3 32.5 %collective-permute-done.2 = bf16[96,9216]{1,0:T(8,128)(2,1)} collective-permute-done((bf16[96,9216]{1,0:T(8,128)(2,1)}, bf16[96,9216]{1,0:T(8,128)(2,1)}, u32[]{:S(2)}, u32[]{:S(2)}) %collective-permute-start.2) | collective-permute-done | bytes 1769504 | tf_op jit(solution)/shard_map/ppermute | solution.py:17
  63.9 1.2 collective-permute-done.3
  65.1 4.9 pad_maximum_fusion
  69.9 474.5 %while.10 = (s32[]{:T(128)}, f32[24,3,128]{2,1,0:T(4,128)S(1)}, s32[24]{0:T(128)S(1)}, f32[4,3072]{1,0:T(4,128)S(1)}, s32[24,5]{0,1:T(8,128)S(1)}, /*index=5*/s3...) while((s32[]{:T(128)}, f32[24,3,128]{2,1,0:T(4,128)S(1)}, ...), condition=%wide.region_22.23_spmd, body=%wide.region_1.22_spmd.sunk | while | flops 149837072 | bytes 25397148 | solution.py:84
  80.3 1.2 fusion.84
  82.7 1.2 fusion.82
  85.0 1.2 fusion.80
  87.3 1.2 fusion.78
  100.1 1.2 fusion.84
  102.4 1.2 fusion.82
  104.8 1.2 fusion.80
  107.1 1.2 fusion.78
  119.9 1.2 fusion.84
  122.2 1.2 fusion.82
  124.5 1.2 fusion.80
  139.6 1.2 fusion.84
  142.0 1.2 fusion.82
  144.3 1.2 fusion.80
  146.7 1.2 fusion.78
  159.4 1.2 fusion.84
  161.7 1.2 fusion.82
  166.4 1.2 fusion.78
  179.2 1.2 fusion.84
  181.5 1.2 fusion.82
  544.5 1.7 copy.187
  546.2 65.4 %reduce-scatter.4.cloned.1.call-done = f32[192,3]{1,0:T(8,128)} async-done(((f32[3072,3]{1,0:T(8,128)}), f32[192,3]{1,0:T(8,128)}) %reduce-scatter.4.cloned.1.call-update) | async-done | bytes 2320
  611.6 1.6 copy.188
  (1220 shorter events, 290.0 us)
Async XLA Ops:
  6.5 24.7 %copy-start.1 = (f32[3,3072]{1,0:T(4,128)S(1)}, f32[3,3072]{1,0:T(4,128)}, u32[]{:S(2)}) copy-start(f32[3,3072]{1,0:T(4,128)} %param.10) | copy-start | bytes 110596
  6.5 58.5 %copy-start = (bf16[96,9216]{1,0:T(8,128)(2,1)S(1)}, bf16[96,9216]{1,0:T(8,128)(2,1)}, u32[]{:S(2)}) copy-start(bf16[96,9216]{1,0:T(8,128)(2,1)} %param.8) | copy-start | bytes 5308420
  6.5 605.0 %reduce-scatter.4.cloned.1.call-start = ((), (), s32[]{:S(2)}) async-start(), calls=%async_computation.1 | async-start | bytes 1671168
  8.3 22.9 %collective-permute-start = (f32[4,3072]{1,0:T(4,128)S(1)}, f32[4,3072]{1,0:T(4,128)S(1)}, u32[]{:S(2)}, u32[]{:S(2)}) collective-permute-start(f32[4,3072]{1,0:T(4,128)S(1)} %pad_maximum_fusion.2), channel_id=1, source_target_pairs={{0,16},{16,32},{32,48},{48,64},{64,80},{80,96},{96,112},{112,128},... | collective-permute-start | bytes 147464 | tf_op jit(solution)/shard_map/ppermute | solution.py:17
  12.2 19.1 %collective-permute-start.1 = (f32[4,3072]{1,0:T(4,128)S(1)}, f32[4,3072]{1,0:T(4,128)S(1)}, u32[]{:S(2)}, u32[]{:S(2)}) collective-permute-start(f32[4,3072]{1,0:T(4,128)S(1)} %pad_maximum_fusion.2), channel_id=1, source_target_pairs={{16,0},{32,16},{48,32},{64,48},{80,64},{96,80},{112,96},{128,112},... | collective-permute-start | bytes 147464 | tf_op jit(solution)/shard_map/ppermute | solution.py:19
  18.0 45.9 %collective-permute-start.2 = (bf16[96,9216]{1,0:T(8,128)(2,1)}, bf16[96,9216]{1,0:T(8,128)(2,1)}, u32[]{:S(2)}, u32[]{:S(2)}) collective-permute-start(bf16[96,9216]{1,0:T(8,128)(2,1)} %param.8), channel_id=1, source_target_pairs={{0,16},{16,32},{32,48},{48,64},{64,80},{80,96},{96,112},{112,128},... | collective-permute-start | bytes 5308424 | tf_op jit(solution)/shard_map/ppermute | solution.py:17
  19.9 45.1 %collective-permute-start.3 = (bf16[96,9216]{1,0:T(8,128)(2,1)}, bf16[96,9216]{1,0:T(8,128)(2,1)}, u32[]{:S(2)}, u32[]{:S(2)}) collective-permute-start(bf16[96,9216]{1,0:T(8,128)(2,1)} %param.8), channel_id=1, source_target_pairs={{16,0},{32,16},{48,32},{64,48},{80,64},{96,80},{112,96},{128,112},... | collective-permute-start | bytes 5308424 | tf_op jit(solution)/shard_map/ppermute | solution.py:19
  31.3 38.6 %copy-start.2 = (s32[24,5]{0,1:T(8,128)S(1)}, s32[24,5]{0,1:T(8,128)}, u32[]{:S(2)}) copy-start(s32[24,5]{0,1:T(8,128)} %param.13) | copy-start | bytes 1444
Sparse Core Ops, SparseCore 0:
  546.3 65.2 reduce-scatter.3
where the time goes:
time: 628 us; the launch traced here: 620 us
  loops' own time  163 us (26%)
  matrix products  142 us (23%)
  local copies, waits for them, and re-layouts  113 us (18%)
  waiting for transfers between devices  99.2 us (16%)
  other arithmetic  70.1 us (11%)
  starting transfers between devices  19.1 us (3%)
  between operations  13.5 us (2%)
    another operation x1, loops' own time, tile_forces(): result = lax.map(one_tile, jnp.arange(count_tiles, dtype=jnp.int32))  163 us
    dot_general x120, matrix products, pair_forces(): lax.dot_general(left, right, (((0,), (0,)), ((), ())), preferred_element_...  142 us
    unnamed x2, waiting for transfers between devices  65.4 us
    reduce_sum x240, other arithmetic, pair_forces(): rows.append(-jnp.sum(term, axis=1))  52.8 us
    slice x120, local copies, waits for them, and re-layouts, pair_forces(): coupling[comp, :, 1, :] * delta[1]  48.9 us
    ppermute x2, waiting for transfers between devices, extended(): lax.ppermute(tail, axis, [(i, (i + 1) % count) for i in range(ends)])  32.6 us
    reshape x120, local copies, waits for them, and re-layouts, pair_forces(): coupling = coupling.reshape(3, tile_size, 3, tile_size)  28.5 us
    dynamic_slice x24, local copies, waits for them, and re-layouts, one_tile(): local = nbr_rows[index, slot] - base_tile  16.4 us
  transfers between devices with their start and end apart: 5, of which 3 were waited for; matrix products, arithmetic and copies ran while one was open for 1% of the time, Pallas kernels for 0%

commit v1 on v0

v1 whole, which is shorter than its diff:
```python
import jax
import jax.numpy as jnp
from jax import lax
from jax.experimental import pallas as pl
from jax.experimental.pallas import tpu as pltpu
from jax.sharding import PartitionSpec as P

BLK = 128
OWN = 24
HALF = 12
LOCAL = OWN + 2 * HALF
SLOTS = 5
DEPTH = 96
WIDTH = 3 * BLK
UNROLL = 4
F32 = jnp.float32
BF16 = jnp.bfloat16


def products(i, j, left, right, out):
    zero = jnp.zeros((DEPTH, BLK), BF16)
    for slot, (a, b, first) in enumerate(((0, 1, True), (0, 2, False), (1, 2, True))):
        col_a, col_b = right[i, a], right[i, b]
        if first:
            diag = jnp.concatenate([col_a * BF16(2), zero], axis=0)
        else:
            diag = jnp.concatenate([zero, col_b * BF16(2)], axis=0)
        rhs = jnp.concatenate([jnp.concatenate([col_b, col_a], axis=0), diag], axis=1)
        res = lax.dot_general(
            left[j, slot], rhs, (((1,), (0,)), ((), ())), preferred_element_type=F32
        )
        out[2 * slot] = res[:, :BLK]
        out[2 * slot + 1] = res[:, BLK:]


def contract(dest, i, j, mats, geo_row, geo_col, acc):
    own = [jnp.broadcast_to(geo_row[i, c : c + 1, :], (8, BLK)) for c in range(4)]
    total = [None, None, None]
    for strip in range(BLK // 8):
        at = pl.ds(8 * strip, 8)
        cols = geo_col[j, at, :]
        other = [jnp.broadcast_to(cols[:, c : c + 1], (8, BLK)) for c in range(4)]
        d = [own[c] - other[c] for c in range(3)]
        s = own[3] + other[3]
        m01, m00, m02, m22, m12, m11 = (mats[k, at, :] for k in range(6))
        u = (d[0] * d[0] + d[1] * d[1]) + (d[2] * d[2] + s * s)
        y = lax.rsqrt(u)
        y2 = y * y
        f5 = y2 * y2 * y
        v0 = m00 * d[0] + m01 * d[1] + m02 * d[2]
        v1 = m01 * d[0] + m11 * d[1] + m12 * d[2]
        v2 = m02 * d[0] + m12 * d[1] + m22 * d[2]
        q = d[0] * v0 + d[1] * v1 + d[2] * v2
        w = (m00 + m11 + m22) * 0.5 - (y2 * 2.5) * q
        for c, v in enumerate((v0, v1, v2)):
            term = f5 * (v + d[c] * w)
            total[c] = term if total[c] is None else total[c] + term
    for c in range(3):
        acc[dest, c] = acc[dest, c] + total[c]


def prepare(tile, src, geo, first, gain, left, right, geo_row, geo_col):
    parts = [
        src[:, pl.ds(pl.multiple_of(first * WIDTH + c * BLK, BLK), BLK)] for c in range(3)
    ]
    for c in range(3):
        right[tile, c] = (parts[c].astype(F32) * gain[...]).astype(BF16)
    for slot, (a, b) in enumerate(((0, 1), (0, 2), (1, 2))):
        left[tile, slot] = jnp.concatenate([parts[a], parts[b]], axis=0).T
    prepare_geo(tile, geo, first, geo_row, geo_col)


def prepare_geo(tile, geo, first, geo_row, geo_col):
    rows = geo[:, pl.ds(pl.multiple_of(first * BLK, BLK), BLK)]
    geo_row[tile] = rows
    geo_col[tile] = jnp.concatenate([rows, jnp.zeros((BLK - 8, BLK), F32)], axis=0).T


def run_pairs(count, pairs, left, right, geo_row, geo_col, mats, acc):
    def fields(code):
        return code // 4096, (code // 64) % 64, code % 64

    trash = LOCAL * 4096 + HALF * 64 + HALF
    for k in range(UNROLL):
        pairs[count + k] = trash
    _, i, j = fields(pairs[0])
    products(i, j, left, right, mats[0])

    @pl.loop(0, (count + UNROLL - 1) // UNROLL)
    def _(step):
        todo = [fields(pairs[step * UNROLL + k]) for k in range(UNROLL + 1)]
        for k in range(UNROLL):
            products(todo[k + 1][1], todo[k + 1][2], left, right, mats[(k + 1) % 2])
            contract(*todo[k], mats[k % 2], geo_row, geo_col, acc)


def append(pairs, count, keep, i, j):
    pairs[count] = i * 4096 + i * 64 + jnp.clip(j, 0, LOCAL - 1)
    return count + keep.astype(jnp.int32)


def own_kernel(
    row, nbr, panel, geo, gain, acc, left, right, pairs, geo_row, geo_col, mat_a, mat_b
):
    acc[...] = jnp.zeros_like(acc)
    shift = HALF - row[0] * OWN

    def scan(index, count):
        i = HALF + index // SLOTS
        j = nbr[index] + shift
        return append(pairs, count, (j >= HALF) & (j < HALF + OWN), i, j)

    count = lax.fori_loop(0, OWN * SLOTS, scan, jnp.int32(0))

    @pl.loop(0, OWN // 2)
    def _(step):
        for k in range(2):
            t = 2 * step + k
            prepare(
                t, panel, geo, t, gain, left, right,
                geo_row.at[pl.ds(HALF, OWN)], geo_col.at[pl.ds(HALF, OWN)],
            )

    class Shifted:
        def __init__(self, ref):
            self.ref = ref

        def __getitem__(self, at):
            return self.ref[(at[0] - HALF,) + at[1:]]

    run_pairs(
        count, pairs, Shifted(left), Shifted(right), geo_row, geo_col, (mat_a, mat_b), acc
    )


def rest_kernel(
    row, nbr, nbr_lo, nbr_hi, start, left_own, right_own, lo, hi, geo, geo_lo, geo_hi, gain,
    out, pairs, acc, left, right, geo_row, geo_col, mat_a, mat_b, sems,
):
    own = pl.ds(HALF, OWN)
    copies = [
        pltpu.make_async_copy(left_own, left.at[own], sems.at[0]),
        pltpu.make_async_copy(right_own, right.at[own], sems.at[1]),
    ]
    for copy in copies:
        copy.start()
    acc[...] = start[...]
    r = row[0]
    shift = HALF - r * OWN

    def scan_own(index, count):
        i = HALF + index // SLOTS
        j = nbr[index] + shift
        low = (j >= 0) & (j < HALF) & (i >= 2 * HALF)
        high = (j >= HALF + OWN) & (j < LOCAL)
        return append(pairs, count, low | high, i, j)

    def scan_lo(index, count):
        j = nbr_lo[index] + shift
        keep = (j >= 2 * HALF) & (j < HALF + OWN) & (r > 0)
        return append(pairs, count, keep, index // SLOTS, j)

    def scan_hi(index, count):
        j = nbr_hi[index] + shift
        keep = (j >= HALF) & (j < HALF + OWN) & (r < 15)
        return append(pairs, count, keep, HALF + OWN + index // SLOTS, j)

    count = lax.fori_loop(0, OWN * SLOTS, scan_own, jnp.int32(0))
    count = lax.fori_loop(0, HALF * SLOTS, scan_lo, count)
    count = lax.fori_loop(0, HALF * SLOTS, scan_hi, count)

    @pl.loop(0, HALF)
    def _(t):
        prepare(t, lo, geo_lo, t, gain, left, right, geo_row, geo_col)
        prepare(HALF + OWN + t, hi, geo_hi, t, gain, left, right, geo_row, geo_col)
        for k in range(2):
            prepare_geo(HALF + 2 * t + k, geo, 2 * t + k, geo_row, geo_col)

    for copy in copies:
        copy.wait()
    run_pairs(count, pairs, left, right, geo_row, geo_col, (mat_a, mat_b), acc)
    for t in range(LOCAL):
        out[t] = -3.0 * jnp.sum(acc[t], axis=1)


VMEM = pl.BlockSpec(memory_space=pltpu.VMEM)
SMEM = pl.BlockSpec(memory_space=pltpu.SMEM)
ANY = pl.BlockSpec(memory_space=pl.ANY)
PARAMS = pltpu.CompilerParams(vmem_limit_bytes=48 << 20)


def stacks(tiles):
    return (tiles, 3, BLK, 2 * DEPTH), (tiles, 3, DEPTH, BLK)


def cost(pairs):
    return pl.CostEstimate(
        flops=pairs * 2 * 3 * BLK * 2 * BLK * 2 * DEPTH, bytes_accessed=8 << 20, transcendentals=0
    )


def own_call(row, nbr, panel, geo, gain):
    left, right = stacks(OWN)
    return pl.pallas_call(
        own_kernel,
        out_shape=(
            jax.ShapeDtypeStruct((LOCAL + 1, 3, 8, BLK), F32),
            jax.ShapeDtypeStruct(left, BF16),
            jax.ShapeDtypeStruct(right, BF16),
        ),
        in_specs=[SMEM, SMEM, VMEM, VMEM, VMEM],
        out_specs=(VMEM, VMEM, VMEM),
        scratch_shapes=[
            pltpu.SMEM((OWN * SLOTS + UNROLL + 4,), jnp.int32),
            pltpu.VMEM((LOCAL, 8, BLK), F32),
            pltpu.VMEM((LOCAL, BLK, BLK), F32),
            pltpu.VMEM((6, BLK, BLK), F32),
            pltpu.VMEM((6, BLK, BLK), F32),
        ],
        compiler_params=PARAMS,
        cost_estimate=cost(40),
        name="own_pairs",
    )(row, nbr, panel, geo, gain)


def rest_call(row, nbr, nbr_lo, nbr_hi, start, left_own, right_own, lo, hi, geo, geo_lo, geo_hi, gain):
    left, right = stacks(LOCAL)
    return pl.pallas_call(
        rest_kernel,
        out_shape=jax.ShapeDtypeStruct((LOCAL, 3, BLK), F32),
        in_specs=[SMEM] * 4 + [VMEM, ANY, ANY] + [VMEM] * 6,
        out_specs=VMEM,
        scratch_shapes=[
            pltpu.SMEM((2 * OWN * SLOTS + UNROLL + 4,), jnp.int32),
            pltpu.VMEM((LOCAL + 1, 3, 8, BLK), F32),
            pltpu.VMEM(left, BF16),
            pltpu.VMEM(right, BF16),
            pltpu.VMEM((LOCAL, 8, BLK), F32),
            pltpu.VMEM((LOCAL, BLK, BLK), F32),
            pltpu.VMEM((6, BLK, BLK), F32),
            pltpu.VMEM((6, BLK, BLK), F32),
            pltpu.SemaphoreType.DMA((2,)),
        ],
        compiler_params=PARAMS,
        cost_estimate=cost(80),
        name="rest_pairs",
    )(row, nbr, nbr_lo, nbr_hi, start, left_own, right_own, lo, hi, geo, geo_lo, geo_hi, gain)


def atom_radius(elements, radii):
    table = (elements[None, :] == jnp.arange(radii.shape[0], dtype=jnp.int32)[:, None]).astype(F32)
    return jnp.sum(table * radii[:, None], axis=0)


def per_device(panel, eigenvalues, positions, elements, radii, neighbors):
    rows = lax.axis_size("row")
    up = [(k, k + 1) for k in range(rows - 1)]
    down = [(k + 1, k) for k in range(rows - 1)]
    atoms = HALF * BLK
    nbr = neighbors.reshape(-1)
    near = HALF * SLOTS

    radius = atom_radius(elements, radii)
    listed = jnp.pad(nbr.astype(F32).reshape(2, near), ((0, 0), (0, atoms - near))).reshape(1, -1)
    geo = jnp.concatenate([positions, radius[None, :], listed, jnp.zeros((3, 2 * atoms), F32)], axis=0)
    geo_lo = lax.ppermute(geo[:, atoms:], "row", up)
    geo_hi = lax.ppermute(geo[:, :atoms], "row", down)
    lo = lax.ppermute(panel[:, HALF * WIDTH :], "row", up)
    hi = lax.ppermute(panel[:, : HALF * WIDTH], "row", down)

    gain = jnp.broadcast_to((0.25 / jnp.sqrt(eigenvalues))[:, None], (DEPTH, BLK))
    row = lax.axis_index("row").astype(jnp.int32).reshape(1)
    start, left_own, right_own = own_call(row, nbr, panel, geo, gain)
    nbr_lo = geo_lo[4, :near].astype(jnp.int32)
    nbr_hi = geo_hi[4, :near].astype(jnp.int32)
    forces = rest_call(
        row, nbr, nbr_lo, nbr_hi, start, left_own, right_own, lo, hi, geo, geo_lo, geo_hi, gain
    )

    from_below = lax.ppermute(forces[HALF + OWN :], "row", up)
    from_above = lax.ppermute(forces[:HALF], "row", down)
    part = forces[HALF : HALF + OWN] + jnp.concatenate([from_below, from_above], axis=0)

    me = lax.axis_index("col")
    cols = lax.axis_size("col")
    for bit in (8, 4, 2, 1):
        if bit == 1:
            part = jnp.transpose(part, (1, 0, 2)).reshape(3, 3 * BLK)
            halves = part[:, : 3 * BLK // 2], part[:, 3 * BLK // 2 :]
        else:
            count = part.shape[0] // 2
            halves = part[:count], part[count:]
        high = (me // bit) % 2 == 1
        sent = jnp.where(high, halves[0], halves[1])
        kept = jnp.where(high, halves[1], halves[0])
        part = kept + lax.ppermute(sent, "col", [(k, k ^ bit) for k in range(cols)])
    return part


def solution(mesh):
    return jax.shard_map(
        per_device,
        mesh=mesh,
        in_specs=(P("col", "row"), P("col"), P(None, "row"), P("row"), P(), P("row", None)),
        out_specs=P(None, ("row", "col")),
        check_vma=False,
    )
```

time: 628 us -> 91.4 us (0.15); the launches traced: 620 us -> 90 us
  loops' own time: 163 us -> 0 us
  matrix products: 142 us -> 0 us
  local copies, waits for them, and re-layouts: 113 us -> 3.51 us
  waiting for transfers between devices: 99.2 us -> 13 us
  other arithmetic: 70.1 us -> 1.01 us
  Pallas kernels: 0 us -> 36.6 us
  starting transfers between devices: 19.1 us -> 35.7 us
  between operations: 13.5 us -> 0.26 us
    another operation x1 -> x0, loops' own time: 163 us -> none  [tile_forces(): result = lax.map(one_tile, jnp.arange(count_tiles, dtype=jnp.int32))]
    dot_general x120 -> x0, matrix products: 142 us -> none  [pair_forces(): lax.dot_general(left, right, (((0,), (0,)), ((), ())), preferred_element_...]
    unnamed x2 -> x0, waiting for transfers between devices: 65.4 us -> none
    reduce_sum x264 -> x0, other arithmetic: 57.3 us -> none  [the longest x240 52.8 us: pair_forces(): rows.append(-jnp.sum(term, axis=1))]
    slice x120 -> x3, local copies, waits for them, and re-layouts: 48.9 us -> 2.96 us  [the longest x1 2.94 us: per_device(): hi = lax.ppermute(panel[:, :HALF * WIDTH], 'row', down)]
    pallas_call x0 -> x2, Pallas kernels: none -> 36.6 us  [the longest x1 25.4 us: rest_call(): pl.pallas_call(rest_kernel, out_shape=jax.ShapeDtypeStruct((LOCAL, 3, BLK...]
    dynamic_slice x72 -> x0, local copies, waits for them, and re-layouts: 31.6 us -> none  [the longest x24 16.4 us: one_tile(): local = nbr_rows[index, slot] - base_tile]
    reshape x120 -> x1, local copies, waits for them, and re-layouts: 28.5 us -> 0.1 us  [per_device(): nbr = neighbors.reshape(-1)]
  transfers between devices with their start and end apart: 5 -> 10, of which waited for: 3 -> 6; matrix products, arithmetic and copies ran while one was open for 1% -> 1% of each run, Pallas kernels for 0% -> 12%
where the time goes in v1:
time: 91.4 us; the launch traced here: 90 us
  Pallas kernels  36.6 us (40%)
  starting transfers between devices  35.7 us (39%)
  waiting for transfers between devices  13 us (14%)
  local copies, waits for them, and re-layouts  3.51 us (4%)
  other arithmetic  1.01 us (1%)
    pallas_call x1, Pallas kernels, rest_call(): pl.pallas_call(rest_kernel, out_shape=jax.ShapeDtypeStruct((LOCAL, 3, BLK...  25.4 us
    pallas_call x1, Pallas kernels, own_call(): pl.pallas_call(own_kernel, out_shape=(jax.ShapeDtypeStruct((LOCAL + 1, 3,...  11.2 us
    ppermute x1, starting transfers between devices, per_device(): hi = lax.ppermute(panel[:, :HALF * WIDTH], 'row', down)  7.7 us
    ppermute x1, starting transfers between devices, per_device(): geo_hi = lax.ppermute(geo[:, :atoms], 'row', down)  7.54 us
    ppermute x1, starting transfers between devices, per_device(): from_above = lax.ppermute(forces[:HALF], 'row', down)  7.54 us
    ppermute x4, starting transfers between devices, per_device(): part = kept + lax.ppermute(sent, 'col', [(k, k ^ bit) for k in range(cols)])  7.14 us
    ppermute x4, waiting for transfers between devices, per_device(): part = kept + lax.ppermute(sent, 'col', [(k, k ^ bit) for k in range(cols)])  7.03 us
    ppermute x1, waiting for transfers between devices, per_device(): geo_lo = lax.ppermute(geo[:, atoms:], 'row', up)  4.46 us
  transfers between devices with their start and end apart: 10, of which 6 were waited for; matrix products, arithmetic and copies ran while one was open for 1% of the time, Pallas kernels for 12%

profile of v1, /device:TPU:4, one launch (start us, length us, event | category | flops | bytes accessed | tf_op | source)
XLA Modules:
  0.0 90.0 jit_solution(11381739311117585105)
XLA Ops:
  0.0 2.9 %fusion.2 = (bf16[96,4608]{1,0:T(8,128)(2,1)}, bf16[96,4608]{1,0:T(8,128)(2,1)}) fusion(bf16[96,9216]{1,0:T(8,128)(2,1)} %panel.1), kind=kLoop, calls=%fused_computation.18 | loop fusion | bytes 3538944 | tf_op jit(solution)/shard_map/slice | solution.py:269
  3.0 7.7 %collective-permute-start.3 = (bf16[96,4608]{1,0:T(8,128)(2,1)}, bf16[96,4608]{1,0:T(8,128)(2,1)S(1)}, u32[]{:S(2)}, u32[]{:S(2)}) collective-permute-start(bf16[96,4608]{1,0:T(8,128)(2,1)} %get-tuple-element.11), channel_id=1, source_target_pairs={{16,0},{32,16},{48,32},{64,48},{80,64},{96,80},{112,96},{128,112},... | collective-permute-start | bytes 2654216 | tf_op jit(solution)/shard_map/ppermute | solution.py:269
  10.7 1.9 %collective-permute-start.2 = (bf16[96,4608]{1,0:T(8,128)(2,1)}, bf16[96,4608]{1,0:T(8,128)(2,1)}, u32[]{:S(2)}, u32[]{:S(2)}) collective-permute-start(bf16[96,4608]{1,0:T(8,128)(2,1)} %get-tuple-element.12), channel_id=1, source_target_pairs={{0,16},{16,32},{32,48},{48,64},{64,80},{80,96},{96,112},{112,128},... | collective-permute-start | bytes 2654216 | tf_op jit(solution)/shard_map/ppermute | solution.py:268
  12.6 0.1 copy.12
  12.7 0.1 convert_element_type.21
  12.8 0.1 pad.10.clone
  12.9 0.1 select_reduce_fusion
  13.0 0.1 maximum_maximum_fusion.geo
  13.1 7.5 %collective-permute-start.1 = (f32[8,1536]{1,0:T(8,128)S(1)}, f32[8,1536]{1,0:T(8,128)S(1)}, u32[]{:S(2)}, u32[]{:S(2)}) collective-permute-start(f32[8,1536]{1,0:T(8,128)S(1)} %get-tuple-element.15), channel_id=1, source_target_pairs={{16,0},{32,16},{48,32},{64,48},{80,64},{96,80},{112,96},{128,112},... | collective-permute-start | bytes 147464 | tf_op jit(solution)/shard_map/ppermute | solution.py:267
  20.7 1.9 %collective-permute-start = (f32[8,1536]{1,0:T(8,128)S(1)}, f32[8,1536]{1,0:T(8,128)S(1)}, u32[]{:S(2)}, u32[]{:S(2)}) collective-permute-start(f32[8,1536]{1,0:T(8,128)S(1)} %get-tuple-element.16), channel_id=1, source_target_pairs={{0,16},{16,32},{32,48},{48,64},{64,80},{80,96},{96,112},{112,128},... | collective-permute-start | bytes 147464 | tf_op jit(solution)/shard_map/ppermute | solution.py:266
  22.6 0.1 copy.11
  22.7 0.1 reshape.21.nbr
  22.8 0.1 broadcast_in_dim.8.gain
  22.9 11.2 %own_pairs.1 = (f32[49,3,8,128]{3,2,1,0:T(8,128)S(1)}, bf16[24,3,128,192]{3,2,1,0:T(8,128)(2,1)}, bf16[24,3,96,128]{3,2,1,0:T(8,128)(2,1)S(1)}) custom-call(s32[1]{0:T(128)} %bitcast.row, s32[120]{0:T(128)S(1)} %reshape.21.nbr, bf16[96,9216]{1,0:T(8,128)(2,1)S(1)} %copy-done, f32[8,3072]{1,0:T(8,128)S(1)} %maximum_maximum_fusion.geo, ...), custom_call_target="tpu_custom_call" | custom-call | flops 1509949440 | bytes 8388608 | tf_op jit(solution)/shard_map/own_pairs/pallas_call | solution.py:204
  34.1 0.0 collective-permute-done.1.geo_hi
  34.1 4.5 %collective-permute-done.geo_lo = f32[8,1536]{1,0:T(8,128)S(1)} collective-permute-done((f32[8,1536]{1,0:T(8,128)S(1)}, f32[8,1536]{1,0:T(8,128)S(1)}, u32[]{:S(2)}, u32[]{:S(2)}) %collective-permute-start) | collective-permute-done | bytes 49184 | tf_op jit(solution)/shard_map/ppermute | solution.py:266
  38.6 0.0 collective-permute-done.3.hi
  38.6 25.4 %rest_pairs.1 = f32[48,3,128]{2,1,0:T(4,128)S(1)} custom-call(s32[1]{0:T(128)} %bitcast.row, s32[120]{0:T(128)S(1)} %reshape.21.nbr, s32[60]{0:T(128)S(1)} %fusion.1.nbr_lo, s32[60]{0:T(128)S(1)} %fusion.nbr_hi, f32[49,3,8,128]{3,2,1,0:T(8,128)S(1)} %get-tuple-element.8.start, bf16[24,3,128,192]{3,2,1,0:T(8,128)(2,1)} %get-tuple-element.9.left_own, ...), custom_call_target="tpu_custom_call" | custom-call | flops 3019898880 | bytes 8388608 | tf_op jit(solution)/shard_map/rest_pairs/pallas_call | solution.py:228
  64.0 1.9 %collective-permute-start.4 = (f32[12,3,128]{2,1,0:T(4,128)S(1)}, f32[12,3,128]{2,1,0:T(4,128)S(1)}, u32[]{:S(2)}, u32[]{:S(2)}) collective-permute-start(f32[12,3,128]{2,1,0:T(4,128)S(1)} %get-tuple-element.13), channel_id=1, source_target_pairs={{0,16},{16,32},{32,48},{48,64},{64,80},{80,96},{96,112},{112,128},... | collective-permute-start | bytes 55304 | tf_op jit(solution)/shard_map/ppermute | solution.py:280
  65.9 7.5 %collective-permute-start.5 = (f32[12,3,128]{2,1,0:T(4,128)S(1)}, f32[12,3,128]{2,1,0:T(4,128)S(1)}, u32[]{:S(2)}, u32[]{:S(2)}) collective-permute-start(f32[12,3,128]{2,1,0:T(4,128)S(1)} %get-tuple-element.14), channel_id=1, source_target_pairs={{16,0},{32,16},{48,32},{64,48},{80,64},{96,80},{112,96},{128,112},... | collective-permute-start | bytes 55304 | tf_op jit(solution)/shard_map/ppermute | solution.py:281
  73.5 0.0 collective-permute-done.4
  73.5 1.5 %collective-permute-done.5 = f32[12,3,128]{2,1,0:T(4,128)S(1)} collective-permute-done((f32[12,3,128]{2,1,0:T(4,128)S(1)}, f32[12,3,128]{2,1,0:T(4,128)S(1)}, u32[]{:S(2)}, u32[]{:S(2)}) %collective-permute-start.5) | collective-permute-done | bytes 18464 | tf_op jit(solution)/shard_map/ppermute | solution.py:281
  75.0 3.3 %collective-permute-start.6 = (f32[12,3,128]{2,1,0:T(4,128)S(1)}, f32[12,3,128]{2,1,0:T(4,128)S(1)}, u32[]{:S(2)}, u32[]{:S(2)}) collective-permute-start(f32[12,3,128]{2,1,0:T(4,128)S(1)} %slice_select_fusion), channel_id=1, source_target_pairs={{0,8},{1,9},{2,10},{3,11},{4,12},{5,13},{6,14},{7,15},{8,0},{9,1},... | collective-permute-start | bytes 55304 | tf_op jit(solution)/shard_map/ppermute | solution.py:296
  78.3 2.1 %collective-permute-done.6 = f32[12,3,128]{2,1,0:T(4,128)S(1)} collective-permute-done((f32[12,3,128]{2,1,0:T(4,128)S(1)}, f32[12,3,128]{2,1,0:T(4,128)S(1)}, u32[]{:S(2)}, u32[]{:S(2)}) %collective-permute-start.6) | collective-permute-done | bytes 18464 | tf_op jit(solution)/shard_map/ppermute | solution.py:296
  80.4 1.7 %collective-permute-start.7 = (f32[6,3,128]{2,1,0:T(4,128)S(1)}, f32[6,3,128]{2,1,0:T(4,128)S(1)}, u32[]{:S(2)}, u32[]{:S(2)}) collective-permute-start(f32[6,3,128]{2,1,0:T(4,128)S(1)} %slice_select_fusion.1), channel_id=1, source_target_pairs={{0,4},{1,5},{2,6},{3,7},{4,0},{5,1},{6,2},{7,3},{8,12},{9,13},{10,... | collective-permute-start | bytes 27656 | tf_op jit(solution)/shard_map/ppermute | solution.py:296
  82.1 2.1 %collective-permute-done.7 = f32[6,3,128]{2,1,0:T(4,128)S(1)} collective-permute-done((f32[6,3,128]{2,1,0:T(4,128)S(1)}, f32[6,3,128]{2,1,0:T(4,128)S(1)}, u32[]{:S(2)}, u32[]{:S(2)}) %collective-permute-start.7) | collective-permute-done | bytes 9248 | tf_op jit(solution)/shard_map/ppermute | solution.py:296
  84.2 2.2 %collective-permute-start.8 = (f32[3,3,128]{2,1,0:T(4,128)S(1)}, f32[3,3,128]{2,1,0:T(4,128)S(1)}, u32[]{:S(2)}, u32[]{:S(2)}) collective-permute-start(f32[3,3,128]{2,1,0:T(4,128)S(1)} %slice_select_fusion.2), channel_id=1, source_target_pairs={{0,2},{1,3},{2,0},{3,1},{4,6},{5,7},{6,4},{7,5},{8,10},{9,11},{10,... | collective-permute-start | bytes 13832 | tf_op jit(solution)/shard_map/ppermute | solution.py:296
  86.4 1.6 %collective-permute-done.8 = f32[3,3,128]{2,1,0:T(4,128)S(1)} collective-permute-done((f32[3,3,128]{2,1,0:T(4,128)S(1)}, f32[3,3,128]{2,1,0:T(4,128)S(1)}, u32[]{:S(2)}, u32[]{:S(2)}) %collective-permute-start.8) | collective-permute-done | bytes 4640 | tf_op jit(solution)/shard_map/ppermute | solution.py:296
  88.0 0.1 slice_select_fusion.3
  88.1 0.0 collective-permute-start.9
  88.1 1.2 %collective-permute-done.9 = f32[3,192]{1,0:T(4,128)S(1)} collective-permute-done((f32[3,192]{1,0:T(4,128)S(1)}, f32[3,192]{1,0:T(4,128)S(1)}, u32[]{:S(2)}, u32[]{:S(2)}) %collective-permute-start.9) | collective-permute-done | bytes 2336 | tf_op jit(solution)/shard_map/ppermute | solution.py:296
  89.3 0.7 select_add_fusion.2
  (29 shorter events, 0.2 us)
Async XLA Ops:
  0.0 22.9 %copy-start = (bf16[96,9216]{1,0:T(8,128)(2,1)S(1)}, bf16[96,9216]{1,0:T(8,128)(2,1)}, u32[]{:S(2)}) copy-start(bf16[96,9216]{1,0:T(8,128)(2,1)} %panel.1) | copy-start | bytes 5308420
  0.0 12.6 %copy-start.2 = (s32[24,5]{0,1:T(8,128)S(1)}, s32[24,5]{0,1:T(8,128)}, u32[]{:S(2)}) copy-start(s32[24,5]{0,1:T(8,128)} %param.11) | copy-start | bytes 1444
  0.0 12.9 %copy-start.4 = (f32[5]{0:T(128)S(1)}, f32[5]{0:T(128)}, u32[]{:S(2)}) copy-start(f32[5]{0:T(128)} %param.10) | copy-start | bytes 64
  0.0 12.9 %copy-start.3 = (s32[3072]{0:T(1024)S(1)}, s32[3072]{0:T(1024)}, u32[]{:S(2)}) copy-start(s32[3072]{0:T(1024)} %param.9) | copy-start | bytes 36868
  0.0 13.0 %copy-start.1 = (f32[3,3072]{1,0:T(4,128)S(1)}, f32[3,3072]{1,0:T(4,128)}, u32[]{:S(2)}) copy-start(f32[3,3072]{1,0:T(4,128)} %param.8) | copy-start | bytes 110596
  0.0 22.8 %copy-start.5 = (f32[96]{0:T(128)S(1)}, f32[96]{0:T(128)}, u32[]{:S(2)}) copy-start(f32[96]{0:T(128)} %param.7) | copy-start | bytes 1156
  3.0 35.6 %collective-permute-start.3 = (bf16[96,4608]{1,0:T(8,128)(2,1)}, bf16[96,4608]{1,0:T(8,128)(2,1)S(1)}, u32[]{:S(2)}, u32[]{:S(2)}) collective-permute-start(bf16[96,4608]{1,0:T(8,128)(2,1)} %get-tuple-element.11), channel_id=1, source_target_pairs={{16,0},{32,16},{48,32},{64,48},{80,64},{96,80},{112,96},{128,112},... | collective-permute-start | bytes 2654216 | tf_op jit(solution)/shard_map/ppermute | solution.py:269
  10.7 27.9 %collective-permute-start.2 = (bf16[96,4608]{1,0:T(8,128)(2,1)}, bf16[96,4608]{1,0:T(8,128)(2,1)}, u32[]{:S(2)}, u32[]{:S(2)}) collective-permute-start(bf16[96,4608]{1,0:T(8,128)(2,1)} %get-tuple-element.12), channel_id=1, source_target_pairs={{0,16},{16,32},{32,48},{48,64},{64,80},{80,96},{96,112},{112,128},... | collective-permute-start | bytes 2654216 | tf_op jit(solution)/shard_map/ppermute | solution.py:268
  13.1 21.0 %collective-permute-start.1 = (f32[8,1536]{1,0:T(8,128)S(1)}, f32[8,1536]{1,0:T(8,128)S(1)}, u32[]{:S(2)}, u32[]{:S(2)}) collective-permute-start(f32[8,1536]{1,0:T(8,128)S(1)} %get-tuple-element.15), channel_id=1, source_target_pairs={{16,0},{32,16},{48,32},{64,48},{80,64},{96,80},{112,96},{128,112},... | collective-permute-start | bytes 147464 | tf_op jit(solution)/shard_map/ppermute | solution.py:267
  20.7 17.9 %collective-permute-start = (f32[8,1536]{1,0:T(8,128)S(1)}, f32[8,1536]{1,0:T(8,128)S(1)}, u32[]{:S(2)}, u32[]{:S(2)}) collective-permute-start(f32[8,1536]{1,0:T(8,128)S(1)} %get-tuple-element.16), channel_id=1, source_target_pairs={{0,16},{16,32},{32,48},{48,64},{64,80},{80,96},{96,112},{112,128},... | collective-permute-start | bytes 147464 | tf_op jit(solution)/shard_map/ppermute | solution.py:266
  64.0 9.5 %collective-permute-start.4 = (f32[12,3,128]{2,1,0:T(4,128)S(1)}, f32[12,3,128]{2,1,0:T(4,128)S(1)}, u32[]{:S(2)}, u32[]{:S(2)}) collective-permute-start(f32[12,3,128]{2,1,0:T(4,128)S(1)} %get-tuple-element.13), channel_id=1, source_target_pairs={{0,16},{16,32},{32,48},{48,64},{64,80},{80,96},{96,112},{112,128},... | collective-permute-start | bytes 55304 | tf_op jit(solution)/shard_map/ppermute | solution.py:280
  65.9 9.0 %collective-permute-start.5 = (f32[12,3,128]{2,1,0:T(4,128)S(1)}, f32[12,3,128]{2,1,0:T(4,128)S(1)}, u32[]{:S(2)}, u32[]{:S(2)}) collective-permute-start(f32[12,3,128]{2,1,0:T(4,128)S(1)} %get-tuple-element.14), channel_id=1, source_target_pairs={{16,0},{32,16},{48,32},{64,48},{80,64},{96,80},{112,96},{128,112},... | collective-permute-start | bytes 55304 | tf_op jit(solution)/shard_map/ppermute | solution.py:281
  75.0 5.4 %collective-permute-start.6 = (f32[12,3,128]{2,1,0:T(4,128)S(1)}, f32[12,3,128]{2,1,0:T(4,128)S(1)}, u32[]{:S(2)}, u32[]{:S(2)}) collective-permute-start(f32[12,3,128]{2,1,0:T(4,128)S(1)} %slice_select_fusion), channel_id=1, source_target_pairs={{0,8},{1,9},{2,10},{3,11},{4,12},{5,13},{6,14},{7,15},{8,0},{9,1},... | collective-permute-start | bytes 55304 | tf_op jit(solution)/shard_map/ppermute | solution.py:296
  80.4 3.8 %collective-permute-start.7 = (f32[6,3,128]{2,1,0:T(4,128)S(1)}, f32[6,3,128]{2,1,0:T(4,128)S(1)}, u32[]{:S(2)}, u32[]{:S(2)}) collective-permute-start(f32[6,3,128]{2,1,0:T(4,128)S(1)} %slice_select_fusion.1), channel_id=1, source_target_pairs={{0,4},{1,5},{2,6},{3,7},{4,0},{5,1},{6,2},{7,3},{8,12},{9,13},{10,... | collective-permute-start | bytes 27656 | tf_op jit(solution)/shard_map/ppermute | solution.py:296
  84.2 3.8 %collective-permute-start.8 = (f32[3,3,128]{2,1,0:T(4,128)S(1)}, f32[3,3,128]{2,1,0:T(4,128)S(1)}, u32[]{:S(2)}, u32[]{:S(2)}) collective-permute-start(f32[3,3,128]{2,1,0:T(4,128)S(1)} %slice_select_fusion.2), channel_id=1, source_target_pairs={{0,2},{1,3},{2,0},{3,1},{4,6},{5,7},{6,4},{7,5},{8,10},{9,11},{10,... | collective-permute-start | bytes 13832 | tf_op jit(solution)/shard_map/ppermute | solution.py:296
  88.1 1.2 %collective-permute-start.9 = (f32[3,192]{1,0:T(4,128)S(1)}, f32[3,192]{1,0:T(4,128)S(1)}, u32[]{:S(2)}, u32[]{:S(2)}) collective-permute-start(f32[3,192]{1,0:T(4,128)S(1)} %slice_select_fusion.3), channel_id=1, source_target_pairs={{0,1},{1,0},{2,3},{3,2},{4,5},{5,4},{6,7},{7,6},{8,9},{9,8},{10,11... | collective-permute-start | bytes 6920 | tf_op jit(solution)/shard_map/ppermute | solution.py:296

commit v2 on v1

v2 whole, which is shorter than its diff:
```python
import functools

import jax
import jax.numpy as jnp
from jax import lax
from jax.experimental import pallas as pl
from jax.experimental.pallas import tpu as pltpu
from jax.sharding import PartitionSpec as P

BLK = 128
OWN = 24
HALF = 12
TRASH = 2 * OWN
LOCAL = OWN + 2 * HALF
SLOTS = 5
DEPTH = 96
WIDTH = 3 * BLK
UNROLL = 4
F32 = jnp.float32
BF16 = jnp.bfloat16


def products(i, j, left, right, out):
    zero = jnp.zeros((DEPTH, BLK), BF16)
    for slot, (a, b, first) in enumerate(((0, 1, True), (0, 2, False), (1, 2, True))):
        col_a, col_b = right[i, a], right[i, b]
        if first:
            diag = jnp.concatenate([col_a * BF16(2), zero], axis=0)
        else:
            diag = jnp.concatenate([zero, col_b * BF16(2)], axis=0)
        rhs = jnp.concatenate([jnp.concatenate([col_b, col_a], axis=0), diag], axis=1)
        res = lax.dot_general(
            left[j, slot], rhs, (((1,), (0,)), ((), ())), preferred_element_type=F32
        )
        out[2 * slot] = res[:, :BLK]
        out[2 * slot + 1] = res[:, BLK:]


def contract(dest, i, j, mats, geo_row, geo_col, acc, back=None, turned=None):
    own = [jnp.broadcast_to(geo_row[i, c : c + 1, :], (8, BLK)) for c in range(4)]
    total = [None, None, None]
    for strip in range(BLK // 8):
        at = pl.ds(8 * strip, 8)
        cols = geo_col[j, at, :]
        other = [jnp.broadcast_to(cols[:, c : c + 1], (8, BLK)) for c in range(4)]
        d = [own[c] - other[c] for c in range(3)]
        s = own[3] + other[3]
        m01, m00, m02, m22, m12, m11 = (mats[k, at, :] for k in range(6))
        u = (d[0] * d[0] + d[1] * d[1]) + (d[2] * d[2] + s * s)
        y = lax.rsqrt(u)
        y2 = y * y
        f5 = y2 * y2 * y
        v0 = m00 * d[0] + m01 * d[1] + m02 * d[2]
        v1 = m01 * d[0] + m11 * d[1] + m12 * d[2]
        v2 = m02 * d[0] + m12 * d[1] + m22 * d[2]
        q = d[0] * v0 + d[1] * v1 + d[2] * v2
        w = (m00 + m11 + m22) * 0.5 - (y2 * 2.5) * q
        terms = [f5 * (v + d[c] * w) for c, v in enumerate((v0, v1, v2))]
        for c, term in enumerate(terms):
            total[c] = term if total[c] is None else total[c] + term
        if turned is not None:
            for c, term in enumerate(terms):
                turned[c, at, :] = term
    for c in range(3):
        acc[dest, c] = acc[dest, c] + total[c]
    if turned is not None:
        for c in range(3):
            flipped = jnp.sum(turned[c].T.reshape(BLK // 8, 8, BLK), axis=0)
            acc[back, c] = acc[back, c] - flipped


def split(src, first):
    at = pl.multiple_of(first * WIDTH, BLK)
    return [src[:, pl.ds(at + c * BLK, BLK)] for c in range(3)]


def turn_parts(tile, parts, left):
    for slot, (a, b) in enumerate(((0, 1), (0, 2), (1, 2))):
        left[tile, slot] = jnp.concatenate([parts[a], parts[b]], axis=0).T


def turned_geo(rows):
    return jnp.concatenate([rows, jnp.zeros((BLK - 8, BLK), F32)], axis=0).T


def encode(dest, back, i, j):
    return dest * 32768 + back * 512 + i * 16 + j


def decode(code):
    return code >> 15, (code >> 9) & 63, (code >> 4) & 31, code & 15


def steps(count, todo_of, left, right, geo_row, geo_col, mats, acc, turned=None, before=None):
    _, _, i, j = todo_of(jnp.int32(0))
    products(i, j, left, right, mats[0])

    def body(step, carry):
        if before is not None:
            carry = before(step, carry)
        todo = [todo_of(step * UNROLL + k) for k in range(UNROLL + 1)]
        for k in range(UNROLL):
            products(todo[k + 1][2], todo[k + 1][3], left, right, mats[(k + 1) % 2])
            dest, back, i, j = todo[k]
            turn = None if turned is None else turned[k % 2]
            contract(dest, i, j, mats[k % 2], geo_row, geo_col, acc, back, turn)
        return carry

    return lax.fori_loop(0, (count + UNROLL - 1) // UNROLL, body, jnp.int32(0))


def pack_kernel(
    panel_hbm, positions_hbm, elements_hbm, radii_hbm, nbr_hbm, geo, lower, upper,
    panel, ext, positions, elements, radii, nbr, sems,
):
    width = HALF * WIDTH
    small = [
        pltpu.make_async_copy(src, dst, sems.at[k])
        for k, (src, dst) in enumerate(
            ((positions_hbm, positions), (elements_hbm, elements), (radii_hbm, radii), (nbr_hbm, nbr))
        )
    ]
    halves = [
        pltpu.make_async_copy(
            panel_hbm.at[:, pl.ds(width * k, width)], panel.at[:, pl.ds(width * k, width)], sems.at[4 + k]
        )
        for k in range(2)
    ]
    for copy in small + [halves[1], halves[0]]:
        copy.start()
    for copy in small:
        copy.wait()
    kinds = elements[...]
    radius = jnp.zeros((OWN, BLK), F32)
    for kind in range(radii.shape[1]):
        radius = jnp.where(kinds == kind, radii[0:1, kind : kind + 1], radius)
    listed = nbr[...].astype(F32)
    listed = jnp.concatenate([listed, jnp.zeros((SLOTS, BLK - OWN), F32)], axis=1)
    listed = jnp.concatenate([listed, jnp.zeros((BLK - SLOTS, BLK), F32)], axis=0).T
    copies = []
    for k, out in ((1, upper), (0, lower)):
        tiles = []
        for t in range(HALF * k, HALF * k + HALF):
            rows = jnp.concatenate(
                [
                    positions[:, t * BLK : (t + 1) * BLK],
                    radius[t : t + 1],
                    listed[t : t + 1],
                    jnp.zeros((3, BLK), F32),
                ],
                axis=0,
            )
            geo[t] = rows
            tiles.append(rows)
        rest = jnp.concatenate(tiles, axis=0)
        for part in range(3):
            coarse = rest.astype(BF16)
            rest = rest - coarse.astype(F32)
            ext[k, :, part * BLK : (part + 1) * BLK] = coarse
        copies.append(
            pltpu.make_async_copy(ext.at[k], out.at[:, pl.ds(width, WIDTH)], sems.at[6 + k])
        )
        copies[-1].start()
    for k, out in ((1, upper), (0, lower)):
        halves[k].wait()
        copies.append(
            pltpu.make_async_copy(
                panel.at[:, pl.ds(width * k, width)], out.at[:, pl.ds(0, width)], sems.at[8 + k]
            )
        )
        copies[-1].start()
    for copy in copies:
        copy.wait()


def own_kernel(
    row, panel, geo, gain, out, right, left, geo_col, pairs, near, near_all, acc, mat_a, mat_b, sem
):
    near_all[...] = geo[:, 4, :].astype(jnp.int32)
    fetch = pltpu.make_async_copy(near_all, near, sem.at[0])
    fetch.start()
    acc[...] = jnp.zeros_like(acc)
    fetch.wait()
    first = row[0] * OWN

    def step(index, count):
        for k in range(3):
            t = 3 * index + k
            parts = split(panel, t)
            turn_parts(t, parts, left)
            for c in range(3):
                right[t, c] = (parts[c].astype(F32) * gain[...]).astype(BF16)
            geo_col[t] = turned_geo(geo[t])
            for slot in range(SLOTS):
                j = near[t, slot] - first
                pairs[count] = encode(t, 0, t, 0) + j
                count = count + ((j >= 0) & (j < OWN)).astype(jnp.int32)
        return count

    def todo_of(n):
        code = pairs[n]
        dest = code >> 15
        return dest, 0, jnp.minimum(dest, OWN - 1), (code & 511) - 16 * jnp.minimum(dest, OWN - 1)

    count = lax.fori_loop(0, OWN // 3, step, jnp.int32(0))
    for k in range(UNROLL):
        pairs[count + k] = encode(OWN, 0, OWN - 1, 0)
    steps(count, todo_of, left, right, geo, geo_col, (mat_a, mat_b), acc)
    out[...] = acc[pl.ds(0, OWN)]


def side_kernel(high, row, start, right, message, geo, out, *scratch):
    pairs, near, near_all, acc, left, geo_col, turn_a, turn_b, mat_a, mat_b, sem = scratch
    width = HALF * WIDTH
    rows = [message[:, width + k * BLK : width + (k + 1) * BLK].astype(F32) for k in range(3)]
    halo = (rows[0] + rows[1] + rows[2]).reshape(HALF, 8, BLK)
    near_all[pl.ds(0, OWN)] = geo[:, 4, :].astype(jnp.int32)
    near_all[pl.ds(OWN, 16)] = jnp.concatenate(
        [halo[:, 4, :].astype(jnp.int32), jnp.zeros((4, BLK), jnp.int32)], axis=0
    )
    fetch = pltpu.make_async_copy(near_all, near, sem.at[0])
    fetch.start()
    for t in range(HALF):
        geo_col[t] = turned_geo(halo[t])
    if high:
        acc[...] = start[...]
    else:
        acc[pl.ds(0, OWN)] = start[...]
        acc[pl.ds(OWN, OWN + 1)] = jnp.zeros((OWN + 1, 3, 8, BLK), F32)

    @pl.loop(0, HALF // 4)
    def _(step):
        for k in range(4):
            turn_parts(4 * step + k, split(message, 4 * step + k), left)

    r = row[0]
    first = r * OWN
    base = 0 if high else HALF
    exists = (r < 15) if high else (r > 0)

    def facing(n):
        n = jnp.minimum(n, HALF - 1)
        return base + n, OWN + base + n, base + n, n

    def scan(step, count):
        for slot in range(2, SLOTS):
            for k in range(4):
                h = 4 * step + k
                i = near[OWN + h, slot] - first
                pairs[count] = encode(TRASH, OWN + base + h, i, h)
                keep = exists & (i >= base) & (i < OWN)
                count = count + keep.astype(jnp.int32)
                for t in (h, HALF + h) if high else (HALF + h,):
                    j = near[t, slot] - first - (OWN if high else -HALF)
                    pairs[count] = encode(t, TRASH, t, j)
                    count = count + ((j >= 0) & (j < HALF)).astype(jnp.int32)
        return count

    fetch.wait()
    rest = (left, right, geo, geo_col, (mat_a, mat_b), acc, (turn_a, turn_b))
    count = steps(HALF, facing, *rest, before=scan)
    for k in range(UNROLL):
        pairs[count + k] = encode(TRASH, TRASH, 0, 0)
    steps(count, lambda n: decode(pairs[n]), *rest)
    if not high:
        out[...] = acc[...]
        return
    for m in range(OWN // 3):
        for part in range(2):
            tiles = []
            for t in range(3 * m, 3 * m + 3):
                tiles.append(-3.0 * jnp.sum(acc[OWN * part + t], axis=1))
            line = jnp.concatenate(tiles, axis=1)
            half = 3 * BLK // 2
            out[2 * m, pl.ds(3 * part, 3)] = line[:, :half]
            out[2 * m + 1, pl.ds(3 * part, 3)] = line[:, half:]


VMEM = pl.BlockSpec(memory_space=pltpu.VMEM)
SMEM = pl.BlockSpec(memory_space=pltpu.SMEM)
ANY = pl.BlockSpec(memory_space=pl.ANY)


def stacks(tiles):
    return (tiles, 3, BLK, 2 * DEPTH), (tiles, 3, DEPTH, BLK)


def cost(pairs):
    return pl.CostEstimate(
        flops=pairs * 2 * 3 * BLK * 2 * BLK * 2 * DEPTH, bytes_accessed=8 << 20, transcendentals=0
    )


def own_call(row, panel, geo, gain):
    left, right = stacks(OWN)
    return pl.pallas_call(
        own_kernel,
        out_shape=(
            jax.ShapeDtypeStruct((OWN, 3, 8, BLK), F32),
            jax.ShapeDtypeStruct(right, BF16),
        ),
        in_specs=[SMEM, VMEM, VMEM, VMEM],
        out_specs=(VMEM, VMEM),
        scratch_shapes=[
            pltpu.VMEM(left, BF16),
            pltpu.VMEM((OWN, BLK, BLK), F32),
            pltpu.SMEM((OWN * SLOTS + UNROLL + 4,), jnp.int32),
            pltpu.SMEM((OWN, BLK), jnp.int32),
            pltpu.VMEM((OWN, BLK), jnp.int32),
            pltpu.VMEM((OWN + 1, 3, 8, BLK), F32),
            pltpu.VMEM((6, BLK, BLK), F32),
            pltpu.VMEM((6, BLK, BLK), F32),
            pltpu.SemaphoreType.DMA((1,)),
        ],
        compiler_params=pltpu.CompilerParams(vmem_limit_bytes=20 << 20),
        cost_estimate=cost(40),
        name="own_pairs",
    )(row, panel, geo, gain)


def side_call(high, *args):
    left, _ = stacks(HALF)
    if high:
        shape = jax.ShapeDtypeStruct((2 * OWN // 3, 6, 3 * BLK // 2), F32)
    else:
        shape = jax.ShapeDtypeStruct((TRASH + 1, 3, 8, BLK), F32)
    return pl.pallas_call(
        functools.partial(side_kernel, high),
        out_shape=shape,
        in_specs=[SMEM] + [VMEM] * 4,
        out_specs=VMEM,
        scratch_shapes=[
            pltpu.SMEM((3 * HALF * (SLOTS - 2) + UNROLL + 4,), jnp.int32),
            pltpu.SMEM((OWN + 16, BLK), jnp.int32),
            pltpu.VMEM((OWN + 16, BLK), jnp.int32),
            pltpu.VMEM((TRASH + 1, 3, 8, BLK), F32),
            pltpu.VMEM(left, BF16),
            pltpu.VMEM((HALF, BLK, BLK), F32),
            pltpu.VMEM((3, BLK, BLK), F32),
            pltpu.VMEM((3, BLK, BLK), F32),
            pltpu.VMEM((6, BLK, BLK), F32),
            pltpu.VMEM((6, BLK, BLK), F32),
            pltpu.SemaphoreType.DMA((1,)),
        ],
        compiler_params=pltpu.CompilerParams(vmem_limit_bytes=20 << 20),
        cost_estimate=cost(30),
        name="above_pairs" if high else "below_pairs",
    )(*args)


def pack_call(panel, positions, elements, radii, nbr):
    message = jax.ShapeDtypeStruct((DEPTH, (HALF + 1) * WIDTH), BF16)
    return pl.pallas_call(
        pack_kernel,
        out_shape=(jax.ShapeDtypeStruct((OWN, 8, BLK), F32), message, message),
        in_specs=[ANY] * 5,
        out_specs=(VMEM, ANY, ANY),
        scratch_shapes=[
            pltpu.VMEM(panel.shape, BF16),
            pltpu.VMEM((2, DEPTH, WIDTH), BF16),
            pltpu.VMEM(positions.shape, F32),
            pltpu.VMEM(elements.shape, jnp.int32),
            pltpu.VMEM(radii.shape, F32),
            pltpu.VMEM(nbr.shape, jnp.int32),
            pltpu.SemaphoreType.DMA((10,)),
        ],
        compiler_params=pltpu.CompilerParams(vmem_limit_bytes=56 << 20),
        name="pack",
    )(panel, positions, elements, radii, nbr)


def per_device(panel, eigenvalues, positions, elements, radii, neighbors):
    rows = lax.axis_size("row")
    up = [(k, k + 1) for k in range(rows - 1)]
    down = [(k + 1, k) for k in range(rows - 1)]
    geo, lower, upper = pack_call(
        panel, positions, elements.reshape(OWN, BLK), radii[None], neighbors.T
    )
    lo = lax.ppermute(upper, "row", up)
    hi = lax.ppermute(lower, "row", down)

    gain = jnp.broadcast_to((0.25 / jnp.sqrt(eigenvalues))[:, None], (DEPTH, BLK))
    row = lax.axis_index("row").astype(jnp.int32).reshape(1)
    start, right = own_call(row, panel, geo, gain)
    start = side_call(False, row, start, right, lo, geo)
    forces = side_call(True, row, start, right, hi, geo)

    cols = lax.axis_size("col")
    part = jnp.sum(lax.all_to_all(forces, "col", 0, 0, tiled=True), axis=0)
    back = []
    for k in range(rows):
        for c in range(cols):
            to = k + 1 if c < cols // 2 else k - 1
            if 0 <= to < rows:
                back.append((k * cols + c, to * cols + c))
    return part[:3] + lax.ppermute(part[3:], ("row", "col"), back)


def solution(mesh):
    return jax.shard_map(
        per_device,
        mesh=mesh,
        in_specs=(P("col", "row"), P("col"), P(None, "row"), P("row"), P(), P("row", None)),
        out_specs=P(None, ("row", "col")),
        check_vma=False,
    )
```

time: 91.4 us -> 72.4 us (0.79)
  starting transfers between devices: 35.7 us -> 11.5 us
  blocking collectives: 0 us -> 12.6 us
  Pallas kernels: 36.6 us -> 29.4 us
  waiting for transfers between devices: 13 us -> 16.4 us
  local copies, waits for them, and re-layouts: 3.51 us -> 0.98 us
    ppermute x10 -> x3, starting transfers between devices: 35.7 us -> 11.5 us  [the longest x1 5.8 us: per_device(): hi = lax.ppermute(lower, 'row', down)]
    all_to_all x0 -> x1, blocking collectives: none -> 12.6 us  [per_device(): part = jnp.sum(lax.all_to_all(forces, 'col', 0, 0, tiled=True), axis=0)]
    pallas_call x2 -> x4, Pallas kernels: 36.6 us -> 29.4 us  [the longest x2 16.7 us: side_call(): pl.pallas_call(functools.partial(side_kernel, high), out_shape=shape, in_...]
    ppermute x10 -> x3, waiting for transfers between devices: 13 us -> 16.4 us  [the longest x1 9.18 us: per_device(): lo = lax.ppermute(upper, 'row', up)]
    slice x3 -> x1, local copies, waits for them, and re-layouts: 2.96 us -> 0.01 us  [per_device(): return part[:3] + lax.ppermute(part[3:], ('row', 'col'), back)]
  transfers between devices with their start and end apart: 10 -> 3, of which waited for: 6 -> 2; matrix products, arithmetic and copies ran while one was open for 1% -> 0% of each run, Pallas kernels for 12% -> 23%
where the time goes in v2:
time: 72.4 us; the launch traced here: 71.7 us
  Pallas kernels  29.4 us (41%)
  waiting for transfers between devices  16.4 us (23%)
  blocking collectives  12.6 us (17%)
  starting transfers between devices  11.5 us (16%)
  local copies, waits for them, and re-layouts  0.98 us (1%)
    pallas_call x2, Pallas kernels, side_call(): pl.pallas_call(functools.partial(side_kernel, high), out_shape=shape, in_...  16.7 us
    all_to_all x1, blocking collectives, per_device(): part = jnp.sum(lax.all_to_all(forces, 'col', 0, 0, tiled=True), axis=0)  12.6 us
    pallas_call x1, Pallas kernels, own_call(): pl.pallas_call(own_kernel, out_shape=(jax.ShapeDtypeStruct((OWN, 3, 8, BL...  9.4 us
    ppermute x1, waiting for transfers between devices, per_device(): lo = lax.ppermute(upper, 'row', up)  9.18 us
    ppermute x1, waiting for transfers between devices, per_device(): return part[:3] + lax.ppermute(part[3:], ('row', 'col'), back)  7.19 us
    ppermute x1, starting transfers between devices, per_device(): hi = lax.ppermute(lower, 'row', down)  5.8 us
    ppermute x1, starting transfers between devices, per_device(): lo = lax.ppermute(upper, 'row', up)  3.83 us
    pallas_call x1, Pallas kernels, pack_call(): pl.pallas_call(pack_kernel, out_shape=(jax.ShapeDtypeStruct((OWN, 8, BLK)...  3.33 us
  transfers between devices with their start and end apart: 3, of which 2 were waited for; matrix products, arithmetic and copies ran while one was open for 0% of the time, Pallas kernels for 23%

profile of v2, /device:TPU:4, one launch (start us, length us, event | category | flops | bytes accessed | tf_op | source)
XLA Modules:
  0.0 71.7 jit_solution(6550728625129135829)
XLA Ops:
  0.0 0.0 copy-start
  0.0 0.0 copy-start.2
  0.0 3.3 %pack.1 = (f32[24,8,128]{2,1,0:T(8,128)}, bf16[96,4992]{1,0:T(8,128)(2,1)}, bf16[96,4992]{1,0:T(8,128)(2,1)}) custom-call(bf16[96,9216]{1,0:T(8,128)(2,1)} %panel.1, f32[3,3072]{1,0:T(4,128)} %positions_hbm.1, s32[24,128]{1,0:T(8,128)} %bitcast.4, f32[1,5]{1,0:T(1,128)} %bitcast.6, s32[5,24]{1,0:T(8,128)} %bitcast.5), custom_call_target="tpu_custom_call" | custom-call | tf_op jit(solution)/shard_map/pack/pallas_call | solution.py:353
  3.3 3.8 %collective-permute-start = (bf16[96,4992]{1,0:T(8,128)(2,1)}, bf16[96,4992]{1,0:T(8,128)(2,1)}, u32[]{:S(2)}, u32[]{:S(2)}) collective-permute-start(bf16[96,4992]{1,0:T(8,128)(2,1)} %get-tuple-element.13), channel_id=1, source_target_pairs={{0,16},{16,32},{32,48},{48,64},{64,80},{80,96},{96,112},{112,128},... | collective-permute-start | bytes 2875400 | tf_op jit(solution)/shard_map/ppermute | solution.py:379
  7.2 5.8 %collective-permute-start.1 = (bf16[96,4992]{1,0:T(8,128)(2,1)}, bf16[96,4992]{1,0:T(8,128)(2,1)S(1)}, u32[]{:S(2)}, u32[]{:S(2)}) collective-permute-start(bf16[96,4992]{1,0:T(8,128)(2,1)} %get-tuple-element.14), channel_id=1, source_target_pairs={{16,0},{32,16},{48,32},{64,48},{80,64},{96,80},{112,96},{128,112},... | collective-permute-start | bytes 2875400 | tf_op jit(solution)/shard_map/ppermute | solution.py:380
  13.0 0.0 copy-done.2
  13.0 0.1 broadcast_in_dim.10.gain
  13.1 0.0 copy-done
  13.1 0.0 copy-start.1
  13.1 0.9 %copy-done.1 = f32[24,8,128]{2,1,0:T(8,128)S(1)} copy-done((f32[24,8,128]{2,1,0:T(8,128)S(1)}, f32[24,8,128]{2,1,0:T(8,128)}, u32[]{:S(2)}) %copy-start.1) | copy-done | bytes 98328
  14.0 9.4 %own_pairs.1 = (f32[24,3,8,128]{3,2,1,0:T(8,128)S(1)}, bf16[24,3,96,128]{3,2,1,0:T(8,128)(2,1)S(1)}) custom-call(s32[1]{0:T(128)} %bitcast.row, bf16[96,9216]{1,0:T(8,128)(2,1)S(1)} %copy-done, f32[24,8,128]{2,1,0:T(8,128)S(1)} %copy-done.1, f32[96,128]{1,0:T(8,128)S(1)} %broadcast_in_dim.10.gain), custom_call_target="tpu_custom_call" | custom-call | flops 1509949440 | bytes 8388608 | tf_op jit(solution)/shard_map/own_pairs/pallas_call | solution.py:296
  23.4 9.2 %collective-permute-done.message = bf16[96,4992]{1,0:T(8,128)(2,1)} collective-permute-done((bf16[96,4992]{1,0:T(8,128)(2,1)}, bf16[96,4992]{1,0:T(8,128)(2,1)}, u32[]{:S(2)}, u32[]{:S(2)}) %collective-permute-start) | collective-permute-done | bytes 958496 | tf_op jit(solution)/shard_map/ppermute | solution.py:379
  32.6 7.1 %below_pairs.1.start = f32[49,3,8,128]{3,2,1,0:T(8,128)S(1)} custom-call(s32[1]{0:T(128)} %bitcast.row, f32[24,3,8,128]{3,2,1,0:T(8,128)S(1)} %get-tuple-element.11.start, bf16[24,3,96,128]{3,2,1,0:T(8,128)(2,1)S(1)} %get-tuple-element.12.right, bf16[96,4992]{1,0:T(8,128)(2,1)} %collective-permute-done.message, f32[24,8,128]{2,1,0:T(8,128)S(1)} %copy-done.1), custom_call_target="tpu_custom_call" | custom-call | flops 1132462080 | bytes 8388608 | tf_op jit(solution)/shard_map/below_pairs/pallas_call | solution.py:327
  39.7 0.0 collective-permute-done.1.message
  39.7 9.6 %above_pairs.1 = f32[16,6,192]{2,1,0:T(8,128)S(1)} custom-call(s32[1]{0:T(128)} %bitcast.row, f32[49,3,8,128]{3,2,1,0:T(8,128)S(1)} %below_pairs.1.start, bf16[24,3,96,128]{3,2,1,0:T(8,128)(2,1)S(1)} %get-tuple-element.12.right, bf16[96,4992]{1,0:T(8,128)(2,1)S(1)} %collective-permute-done.1.message, f32[24,8,128]{2,1,0:T(8,128)S(1)} %copy-done.1), custom_call_target="tpu_custom_call" | custom-call | flops 1132462080 | bytes 8388608 | tf_op jit(solution)/shard_map/above_pairs/pallas_call | solution.py:327
  49.3 12.6 %all_to_all.5 = f32[16,6,192]{2,1,0:T(8,128)S(1)} all-to-all(f32[16,6,192]{2,1,0:T(8,128)S(1)} %above_pairs.1), channel_id=1, replica_groups=mesh['row'=16,'col'=16] {'col'}, dimensions={0} | all-to-all | bytes 147456 | tf_op jit(solution)/shard_map/all_to_all | solution.py:389
  62.0 1.9 %collective-permute-start.2 = (f32[3,192]{1,0:T(4,128)S(1)}, f32[3,192]{1,0:T(4,128)S(1)}, u32[]{:S(2)}, u32[]{:S(2)}) collective-permute-start(f32[3,192]{1,0:T(4,128)S(1)} %slice.9), channel_id=1, source_target_pairs={{0,16},{1,17},{2,18},{3,19},{4,20},{5,21},{6,22},{7,23},{16,32},{1... | collective-permute-start | bytes 6920 | tf_op jit(solution)/shard_map/ppermute | solution.py:396
  63.9 7.2 %collective-permute-done.2 = f32[3,192]{1,0:T(4,128)S(1)} collective-permute-done((f32[3,192]{1,0:T(4,128)S(1)}, f32[3,192]{1,0:T(4,128)S(1)}, u32[]{:S(2)}, u32[]{:S(2)}) %collective-permute-start.2) | collective-permute-done | bytes 2336 | tf_op jit(solution)/shard_map/ppermute | solution.py:396
  71.1 0.6 slice_add_fusion
  (3 shorter events, 0.0 us)
Async XLA Ops:
  0.0 13.1 %copy-start = (bf16[96,9216]{1,0:T(8,128)(2,1)S(1)}, bf16[96,9216]{1,0:T(8,128)(2,1)}, u32[]{:S(2)}) copy-start(bf16[96,9216]{1,0:T(8,128)(2,1)} %panel.1) | copy-start | bytes 5308420
  0.0 13.0 %copy-start.2 = (f32[96]{0:T(128)S(1)}, f32[96]{0:T(128)}, u32[]{:S(2)}) copy-start(f32[96]{0:T(128)} %param.7) | copy-start | bytes 1156
  3.3 29.2 %collective-permute-start = (bf16[96,4992]{1,0:T(8,128)(2,1)}, bf16[96,4992]{1,0:T(8,128)(2,1)}, u32[]{:S(2)}, u32[]{:S(2)}) collective-permute-start(bf16[96,4992]{1,0:T(8,128)(2,1)} %get-tuple-element.13), channel_id=1, source_target_pairs={{0,16},{16,32},{32,48},{48,64},{64,80},{80,96},{96,112},{112,128},... | collective-permute-start | bytes 2875400 | tf_op jit(solution)/shard_map/ppermute | solution.py:379
  7.2 32.5 %collective-permute-start.1 = (bf16[96,4992]{1,0:T(8,128)(2,1)}, bf16[96,4992]{1,0:T(8,128)(2,1)S(1)}, u32[]{:S(2)}, u32[]{:S(2)}) collective-permute-start(bf16[96,4992]{1,0:T(8,128)(2,1)} %get-tuple-element.14), channel_id=1, source_target_pairs={{16,0},{32,16},{48,32},{64,48},{80,64},{96,80},{112,96},{128,112},... | collective-permute-start | bytes 2875400 | tf_op jit(solution)/shard_map/ppermute | solution.py:380
  13.1 0.9 %copy-start.1 = (f32[24,8,128]{2,1,0:T(8,128)S(1)}, f32[24,8,128]{2,1,0:T(8,128)}, u32[]{:S(2)}) copy-start(f32[24,8,128]{2,1,0:T(8,128)} %get-tuple-element.10.geo) | copy-start | bytes 294916
  62.0 9.1 %collective-permute-start.2 = (f32[3,192]{1,0:T(4,128)S(1)}, f32[3,192]{1,0:T(4,128)S(1)}, u32[]{:S(2)}, u32[]{:S(2)}) collective-permute-start(f32[3,192]{1,0:T(4,128)S(1)} %slice.9), channel_id=1, source_target_pairs={{0,16},{1,17},{2,18},{3,19},{4,20},{5,21},{6,22},{7,23},{16,32},{1... | collective-permute-start | bytes 6920 | tf_op jit(solution)/shard_map/ppermute | solution.py:396

commit v3 on v2

--- a/solution.py
+++ b/solution.py
@@ -41,8 +41,7 @@
     total = [None, None, None]
     for strip in range(BLK // 8):
         at = pl.ds(8 * strip, 8)
-        cols = geo_col[j, at, :]
-        other = [jnp.broadcast_to(cols[:, c : c + 1], (8, BLK)) for c in range(4)]
+        other = [geo_col[j, c, at, :] for c in range(4)]
         d = [own[c] - other[c] for c in range(3)]
         s = own[3] + other[3]
         m01, m00, m02, m22, m12, m11 = (mats[k, at, :] for k in range(6))
@@ -83,12 +82,21 @@
     return jnp.concatenate([rows, jnp.zeros((BLK - 8, BLK), F32)], axis=0).T
 
 
-def encode(dest, back, i, j):
-    return dest * 32768 + back * 512 + i * 16 + j
+def encode(dest, back, own, halo):
+    return dest * 32768 + back * 512 + own * 16 + halo
 
 
 def decode(code):
-    return code >> 15, (code >> 9) & 63, (code >> 4) & 31, code & 15
+    return code >> 15, (code >> 9) & 63, code & 15, (code >> 4) & 31
+
+
+class Columns:
+    def __init__(self, ref):
+        self.ref = ref
+
+    def __getitem__(self, at):
+        tile, c = at
+        return self.ref[:, pl.ds(pl.multiple_of(tile * WIDTH + c * BLK, BLK), BLK)]
 
 
 def steps(count, todo_of, left, right, geo_row, geo_col, mats, acc, turned=None, before=None):
@@ -174,7 +182,7 @@
 
 
 def own_kernel(
-    row, panel, geo, gain, out, right, left, geo_col, pairs, near, near_all, acc, mat_a, mat_b, sem
+    row, panel, geo, gain, out, scaled, geo_col, left, right, pairs, near, near_all, acc, mat_a, mat_b, sem
 ):
     near_all[...] = geo[:, 4, :].astype(jnp.int32)
     fetch = pltpu.make_async_copy(near_all, near, sem.at[0])
@@ -188,9 +196,13 @@
             t = 3 * index + k
             parts = split(panel, t)
             turn_parts(t, parts, left)
+            parts = [(part.astype(F32) * gain[...]).astype(BF16) for part in parts]
+            turn_parts(t, parts, scaled)
             for c in range(3):
-                right[t, c] = (parts[c].astype(F32) * gain[...]).astype(BF16)
-            geo_col[t] = turned_geo(geo[t])
+                right[t, c] = parts[c]
+            columns = turned_geo(geo[t])
+            for c in range(4):
+                geo_col[t, c] = jnp.broadcast_to(columns[:, c : c + 1], (BLK, BLK))
             for slot in range(SLOTS):
                 j = near[t, slot] - first
                 pairs[count] = encode(t, 0, t, 0) + j
@@ -209,8 +221,8 @@
     out[...] = acc[pl.ds(0, OWN)]
 
 
-def side_kernel(high, row, start, right, message, geo, out, *scratch):
-    pairs, near, near_all, acc, left, geo_col, turn_a, turn_b, mat_a, mat_b, sem = scratch
+def side_kernel(high, row, start, scaled, geo_col, message, geo, out, *scratch):
+    pairs, near, near_all, acc, halo_row, turn_a, turn_b, mat_a, mat_b, sem = scratch
     width = HALF * WIDTH
     rows = [message[:, width + k * BLK : width + (k + 1) * BLK].astype(F32) for k in range(3)]
     halo = (rows[0] + rows[1] + rows[2]).reshape(HALF, 8, BLK)
@@ -220,19 +232,13 @@
     )
     fetch = pltpu.make_async_copy(near_all, near, sem.at[0])
     fetch.start()
-    for t in range(HALF):
-        geo_col[t] = turned_geo(halo[t])
+    halo_row[...] = halo
     if high:
         acc[...] = start[...]
     else:
         acc[pl.ds(0, OWN)] = start[...]
         acc[pl.ds(OWN, OWN + 1)] = jnp.zeros((OWN + 1, 3, 8, BLK), F32)
 
-    @pl.loop(0, HALF // 4)
-    def _(step):
-        for k in range(4):
-            turn_parts(4 * step + k, split(message, 4 * step + k), left)
-
     r = row[0]
     first = r * OWN
     base = 0 if high else HALF
@@ -240,24 +246,24 @@
 
     def facing(n):
         n = jnp.minimum(n, HALF - 1)
-        return base + n, OWN + base + n, base + n, n
+        return OWN + base + n, base + n, n, base + n
 
     def scan(step, count):
         for slot in range(2, SLOTS):
             for k in range(4):
                 h = 4 * step + k
                 i = near[OWN + h, slot] - first
-                pairs[count] = encode(TRASH, OWN + base + h, i, h)
+                pairs[count] = encode(OWN + base + h, TRASH, i, h)
                 keep = exists & (i >= base) & (i < OWN)
                 count = count + keep.astype(jnp.int32)
                 for t in (h, HALF + h) if high else (HALF + h,):
                     j = near[t, slot] - first - (OWN if high else -HALF)
-                    pairs[count] = encode(t, TRASH, t, j)
+                    pairs[count] = encode(TRASH, t, t, j)
                     count = count + ((j >= 0) & (j < HALF)).astype(jnp.int32)
         return count
 
     fetch.wait()
-    rest = (left, right, geo, geo_col, (mat_a, mat_b), acc, (turn_a, turn_b))
+    rest = (scaled, Columns(message), halo_row, geo_col, (mat_a, mat_b), acc, (turn_a, turn_b))
     count = steps(HALF, facing, *rest, before=scan)
     for k in range(UNROLL):
         pairs[count + k] = encode(TRASH, TRASH, 0, 0)
@@ -297,13 +303,14 @@
         own_kernel,
         out_shape=(
             jax.ShapeDtypeStruct((OWN, 3, 8, BLK), F32),
-            jax.ShapeDtypeStruct(right, BF16),
+            jax.ShapeDtypeStruct(left, BF16),
+            jax.ShapeDtypeStruct((OWN, 4, BLK, BLK), F32),
         ),
         in_specs=[SMEM, VMEM, VMEM, VMEM],
-        out_specs=(VMEM, VMEM),
+        out_specs=(VMEM, VMEM, VMEM),
         scratch_shapes=[
             pltpu.VMEM(left, BF16),
-            pltpu.VMEM((OWN, BLK, BLK), F32),
+            pltpu.VMEM(right, BF16),
             pltpu.SMEM((OWN * SLOTS + UNROLL + 4,), jnp.int32),
             pltpu.SMEM((OWN, BLK), jnp.int32),
             pltpu.VMEM((OWN, BLK), jnp.int32),
@@ -319,7 +326,6 @@
 
 
 def side_call(high, *args):
-    left, _ = stacks(HALF)
     if high:
         shape = jax.ShapeDtypeStruct((2 * OWN // 3, 6, 3 * BLK // 2), F32)
     else:
@@ -327,15 +333,14 @@
     return pl.pallas_call(
         functools.partial(side_kernel, high),
         out_shape=shape,
-        in_specs=[SMEM] + [VMEM] * 4,
+        in_specs=[SMEM] + [VMEM] * 5,
         out_specs=VMEM,
         scratch_shapes=[
             pltpu.SMEM((3 * HALF * (SLOTS - 2) + UNROLL + 4,), jnp.int32),
             pltpu.SMEM((OWN + 16, BLK), jnp.int32),
             pltpu.VMEM((OWN + 16, BLK), jnp.int32),
             pltpu.VMEM((TRASH + 1, 3, 8, BLK), F32),
-            pltpu.VMEM(left, BF16),
-            pltpu.VMEM((HALF, BLK, BLK), F32),
+            pltpu.VMEM((HALF, 8, BLK), F32),
             pltpu.VMEM((3, BLK, BLK), F32),
             pltpu.VMEM((3, BLK, BLK), F32),
             pltpu.VMEM((6, BLK, BLK), F32),
@@ -381,9 +386,9 @@
 
     gain = jnp.broadcast_to((0.25 / jnp.sqrt(eigenvalues))[:, None], (DEPTH, BLK))
     row = lax.axis_index("row").astype(jnp.int32).reshape(1)
-    start, right = own_call(row, panel, geo, gain)
-    start = side_call(False, row, start, right, lo, geo)
-    forces = side_call(True, row, start, right, hi, geo)
+    start, *own = own_call(row, panel, geo, gain)
+    start = side_call(False, row, start, *own, lo, geo)
+    forces = side_call(True, row, start, *own, hi, geo)
 
     cols = lax.axis_size("col")
     part = jnp.sum(lax.all_to_all(forces, "col", 0, 0, tiled=True), axis=0)

time: 72.4 us -> 71.1 us (0.982)
  waiting for transfers between devices: 16.4 us -> 10.7 us
  Pallas kernels: 29.4 us -> 31.8 us
  local copies, waits for them, and re-layouts: 0.98 us -> 2.46 us
    ppermute x1, waiting for transfers between devices: 9.18 us -> 3.46 us  [per_device(): lo = lax.ppermute(upper, 'row', up)]
    pallas_call x1, Pallas kernels: 9.4 us -> 12.9 us  [own_call(): pl.pallas_call(own_kernel, out_shape=(jax.ShapeDtypeStruct((OWN, 3, 8, BL...]
    unnamed x6 -> x4, local copies, waits for them, and re-layouts: 0.9 us -> 2.38 us
    pallas_call x2, Pallas kernels: 16.7 us -> 15.7 us  [side_call(): pl.pallas_call(functools.partial(side_kernel, high), out_shape=shape, in_...]
  transfers between devices with their start and end apart: 3 -> 3, of which waited for: 2 -> 2; matrix products, arithmetic and copies ran while one was open for 0% -> 1% of each run, Pallas kernels for 23% -> 27%
where the time goes in v3:
time: 71.1 us; the launch traced here: 70.4 us
  Pallas kernels  31.8 us (45%)
  blocking collectives  12.6 us (18%)
  starting transfers between devices  11.5 us (16%)
  waiting for transfers between devices  10.7 us (15%)
  local copies, waits for them, and re-layouts  2.46 us (3%)
  other arithmetic  1.28 us (2%)
    pallas_call x2, Pallas kernels, side_call(): pl.pallas_call(functools.partial(side_kernel, high), out_shape=shape, in_...  15.7 us
    pallas_call x1, Pallas kernels, own_call(): pl.pallas_call(own_kernel, out_shape=(jax.ShapeDtypeStruct((OWN, 3, 8, BL...  12.9 us
    all_to_all x1, blocking collectives, per_device(): part = jnp.sum(lax.all_to_all(forces, 'col', 0, 0, tiled=True), axis=0)  12.6 us
    ppermute x1, waiting for transfers between devices, per_device(): return part[:3] + lax.ppermute(part[3:], ('row', 'col'), back)  7.19 us
    ppermute x1, starting transfers between devices, per_device(): hi = lax.ppermute(lower, 'row', down)  5.8 us
    ppermute x1, starting transfers between devices, per_device(): lo = lax.ppermute(upper, 'row', up)  3.83 us
    ppermute x1, waiting for transfers between devices, per_device(): lo = lax.ppermute(upper, 'row', up)  3.46 us
    pallas_call x1, Pallas kernels, pack_call(): pl.pallas_call(pack_kernel, out_shape=(jax.ShapeDtypeStruct((OWN, 8, BLK)...  3.24 us
  transfers between devices with their start and end apart: 3, of which 2 were waited for; matrix products, arithmetic and copies ran while one was open for 1% of the time, Pallas kernels for 27%

profile of v3, /device:TPU:4, one launch (start us, length us, event | category | flops | bytes accessed | tf_op | source)
XLA Modules:
  0.0 70.4 jit_solution(17223423868409471831)
XLA Ops:
  0.0 3.2 %pack.1 = (f32[24,8,128]{2,1,0:T(8,128)}, bf16[96,4992]{1,0:T(8,128)(2,1)}, bf16[96,4992]{1,0:T(8,128)(2,1)}) custom-call(bf16[96,9216]{1,0:T(8,128)(2,1)} %panel.1, f32[3,3072]{1,0:T(4,128)} %positions_hbm.1, s32[24,128]{1,0:T(8,128)} %bitcast.4, f32[1,5]{1,0:T(1,128)} %bitcast.6, s32[5,24]{1,0:T(8,128)} %bitcast.5), custom_call_target="tpu_custom_call" | custom-call | tf_op jit(solution)/shard_map/pack/pallas_call | solution.py:358
  3.2 3.8 %collective-permute-start = (bf16[96,4992]{1,0:T(8,128)(2,1)}, bf16[96,4992]{1,0:T(8,128)(2,1)S(1)}, u32[]{:S(2)}, u32[]{:S(2)}) collective-permute-start(bf16[96,4992]{1,0:T(8,128)(2,1)} %get-tuple-element.15), channel_id=1, source_target_pairs={{0,16},{16,32},{32,48},{48,64},{64,80},{80,96},{96,112},{112,128},... | collective-permute-start | bytes 2875400 | tf_op jit(solution)/shard_map/ppermute | solution.py:384
  7.1 5.8 %collective-permute-start.1 = (bf16[96,4992]{1,0:T(8,128)(2,1)}, bf16[96,4992]{1,0:T(8,128)(2,1)S(1)}, u32[]{:S(2)}, u32[]{:S(2)}) collective-permute-start(bf16[96,4992]{1,0:T(8,128)(2,1)} %get-tuple-element.16), channel_id=1, source_target_pairs={{16,0},{32,16},{48,32},{64,48},{80,64},{96,80},{112,96},{128,112},... | collective-permute-start | bytes 2875400 | tf_op jit(solution)/shard_map/ppermute | solution.py:385
  12.9 0.7 rsqrt_multiply_fusion
  13.6 0.1 broadcast_in_dim.10.gain
  13.6 0.0 copy-start
  13.6 1.5 %copy-done = bf16[96,9216]{1,0:T(8,128)(2,1)S(1)} copy-done((bf16[96,9216]{1,0:T(8,128)(2,1)S(1)}, bf16[96,9216]{1,0:T(8,128)(2,1)}, u32[]{:S(2)}) %copy-start) | copy-done | bytes 1769496
  15.1 0.0 copy-start.1
  15.1 0.9 %copy-done.1 = f32[24,8,128]{2,1,0:T(8,128)S(1)} copy-done((f32[24,8,128]{2,1,0:T(8,128)S(1)}, f32[24,8,128]{2,1,0:T(8,128)}, u32[]{:S(2)}) %copy-start.1) | copy-done | bytes 98328
  16.0 12.9 %own_pairs.1 = (f32[24,3,8,128]{3,2,1,0:T(8,128)S(1)}, bf16[24,3,128,192]{3,2,1,0:T(8,128)(2,1)S(1)}, f32[24,4,128,128]{3,2,1,0:T(8,128)S(1)}) custom-call(s32[1]{0:T(128)} %bitcast.row, bf16[96,9216]{1,0:T(8,128)(2,1)S(1)} %copy-done, f32[24,8,128]{2,1,0:T(8,128)S(1)} %copy-done.1, f32[96,128]{1,0:T(8,128)S(1)} %broadcast_in_dim.10.gain), custom_call_target="tpu_custom_call" | custom-call | flops 1509949440 | bytes 8388608 | tf_op jit(solution)/shard_map/own_pairs/pallas_call | solution.py:302
  28.9 3.5 %collective-permute-done.message = bf16[96,4992]{1,0:T(8,128)(2,1)S(1)} collective-permute-done((bf16[96,4992]{1,0:T(8,128)(2,1)}, bf16[96,4992]{1,0:T(8,128)(2,1)S(1)}, u32[]{:S(2)}, u32[]{:S(2)}) %collective-permute-start) | collective-permute-done | bytes 958496 | tf_op jit(solution)/shard_map/ppermute | solution.py:384
  32.4 6.2 %below_pairs.1.start = f32[49,3,8,128]{3,2,1,0:T(8,128)S(1)} custom-call(s32[1]{0:T(128)} %bitcast.row, f32[24,3,8,128]{3,2,1,0:T(8,128)S(1)} %get-tuple-element.12.start, bf16[24,3,128,192]{3,2,1,0:T(8,128)(2,1)S(1)} %get-tuple-element.13.scaled, f32[24,4,128,128]{3,2,1,0:T(8,128)S(1)} %get-tuple-element.14.geo_col, ...), custom_call_target="tpu_custom_call" | custom-call | flops 1132462080 | bytes 8388608 | tf_op jit(solution)/shard_map/below_pairs/pallas_call | solution.py:333
  38.6 0.0 collective-permute-done.1.message
  38.6 9.5 %above_pairs.1 = f32[16,6,192]{2,1,0:T(8,128)S(1)} custom-call(s32[1]{0:T(128)} %bitcast.row, f32[49,3,8,128]{3,2,1,0:T(8,128)S(1)} %below_pairs.1.start, bf16[24,3,128,192]{3,2,1,0:T(8,128)(2,1)S(1)} %get-tuple-element.13.scaled, f32[24,4,128,128]{3,2,1,0:T(8,128)S(1)} %get-tuple-element.14.geo_col, bf16[96,4992]{1,0:T(8,128)(2,1)S(1)} %collective-permute-done.1.message, ...), custom_call_target="tpu_custom_call" | custom-call | flops 1132462080 | bytes 8388608 | tf_op jit(solution)/shard_map/above_pairs/pallas_call | solution.py:333
  48.1 12.6 %all_to_all.5 = f32[16,6,192]{2,1,0:T(8,128)S(1)} all-to-all(f32[16,6,192]{2,1,0:T(8,128)S(1)} %above_pairs.1), channel_id=1, replica_groups=mesh['row'=16,'col'=16] {'col'}, dimensions={0} | all-to-all | bytes 147456 | tf_op jit(solution)/shard_map/all_to_all | solution.py:394
  60.7 1.9 %collective-permute-start.2 = (f32[3,192]{1,0:T(4,128)S(1)}, f32[3,192]{1,0:T(4,128)S(1)}, u32[]{:S(2)}, u32[]{:S(2)}) collective-permute-start(f32[3,192]{1,0:T(4,128)S(1)} %slice.9), channel_id=1, source_target_pairs={{0,16},{1,17},{2,18},{3,19},{4,20},{5,21},{6,22},{7,23},{16,32},{1... | collective-permute-start | bytes 6920 | tf_op jit(solution)/shard_map/ppermute | solution.py:401
  62.7 7.2 %collective-permute-done.2 = f32[3,192]{1,0:T(4,128)S(1)} collective-permute-done((f32[3,192]{1,0:T(4,128)S(1)}, f32[3,192]{1,0:T(4,128)S(1)}, u32[]{:S(2)}, u32[]{:S(2)}) %collective-permute-start.2) | collective-permute-done | bytes 2336 | tf_op jit(solution)/shard_map/ppermute | solution.py:401
  69.8 0.6 slice_add_fusion
  (2 shorter events, 0.0 us)
Async XLA Ops:
  3.2 29.1 %collective-permute-start = (bf16[96,4992]{1,0:T(8,128)(2,1)}, bf16[96,4992]{1,0:T(8,128)(2,1)S(1)}, u32[]{:S(2)}, u32[]{:S(2)}) collective-permute-start(bf16[96,4992]{1,0:T(8,128)(2,1)} %get-tuple-element.15), channel_id=1, source_target_pairs={{0,16},{16,32},{32,48},{48,64},{64,80},{80,96},{96,112},{112,128},... | collective-permute-start | bytes 2875400 | tf_op jit(solution)/shard_map/ppermute | solution.py:384
  7.1 31.5 %collective-permute-start.1 = (bf16[96,4992]{1,0:T(8,128)(2,1)}, bf16[96,4992]{1,0:T(8,128)(2,1)S(1)}, u32[]{:S(2)}, u32[]{:S(2)}) collective-permute-start(bf16[96,4992]{1,0:T(8,128)(2,1)} %get-tuple-element.16), channel_id=1, source_target_pairs={{16,0},{32,16},{48,32},{64,48},{80,64},{96,80},{112,96},{128,112},... | collective-permute-start | bytes 2875400 | tf_op jit(solution)/shard_map/ppermute | solution.py:385
  13.6 1.5 %copy-start = (bf16[96,9216]{1,0:T(8,128)(2,1)S(1)}, bf16[96,9216]{1,0:T(8,128)(2,1)}, u32[]{:S(2)}) copy-start(bf16[96,9216]{1,0:T(8,128)(2,1)} %panel.1) | copy-start | bytes 5308420
  15.1 0.9 %copy-start.1 = (f32[24,8,128]{2,1,0:T(8,128)S(1)}, f32[24,8,128]{2,1,0:T(8,128)}, u32[]{:S(2)}) copy-start(f32[24,8,128]{2,1,0:T(8,128)} %get-tuple-element.11.geo) | copy-start | bytes 294916
  60.7 9.1 %collective-permute-start.2 = (f32[3,192]{1,0:T(4,128)S(1)}, f32[3,192]{1,0:T(4,128)S(1)}, u32[]{:S(2)}, u32[]{:S(2)}) collective-permute-start(f32[3,192]{1,0:T(4,128)S(1)} %slice.9), channel_id=1, source_target_pairs={{0,16},{1,17},{2,18},{3,19},{4,20},{5,21},{6,22},{7,23},{16,32},{1... | collective-permute-start | bytes 6920 | tf_op jit(solution)/shard_map/ppermute | solution.py:401

commit v4 on v3

--- a/solution.py
+++ b/solution.py
@@ -15,7 +15,7 @@
 SLOTS = 5
 DEPTH = 96
 WIDTH = 3 * BLK
-UNROLL = 4
+UNROLL = 6
 F32 = jnp.float32
 BF16 = jnp.bfloat16
 
@@ -250,8 +250,8 @@
 
     def scan(step, count):
         for slot in range(2, SLOTS):
-            for k in range(4):
-                h = 4 * step + k
+            for k in range(UNROLL):
+                h = UNROLL * step + k
                 i = near[OWN + h, slot] - first
                 pairs[count] = encode(OWN + base + h, TRASH, i, h)
                 keep = exists & (i >= base) & (i < OWN)

time: 71.1 us -> 69.8 us (0.982); the launches traced: 70.4 us -> 70.6 us
  no operation moved by 1% of the time
where the time goes in v4:
time: 69.8 us; the launch traced here: 70.6 us
  Pallas kernels  32.1 us (46%)
  blocking collectives  12.6 us (18%)
  starting transfers between devices  11.5 us (16%)
  waiting for transfers between devices  10.6 us (15%)
  local copies, waits for them, and re-layouts  2.46 us (4%)
  other arithmetic  1.28 us (2%)
    pallas_call x2, Pallas kernels, side_call(): pl.pallas_call(functools.partial(side_kernel, high), out_shape=shape, in_...  15.9 us
    pallas_call x1, Pallas kernels, own_call(): pl.pallas_call(own_kernel, out_shape=(jax.ShapeDtypeStruct((OWN, 3, 8, BL...  13 us
    all_to_all x1, blocking collectives, per_device(): part = jnp.sum(lax.all_to_all(forces, 'col', 0, 0, tiled=True), axis=0)  12.6 us
    ppermute x1, waiting for transfers between devices, per_device(): return part[:3] + lax.ppermute(part[3:], ('row', 'col'), back)  7.19 us
    ppermute x1, starting transfers between devices, per_device(): hi = lax.ppermute(lower, 'row', down)  5.8 us
    ppermute x1, starting transfers between devices, per_device(): lo = lax.ppermute(upper, 'row', up)  3.83 us
    ppermute x1, waiting for transfers between devices, per_device(): lo = lax.ppermute(upper, 'row', up)  3.39 us
    pallas_call x1, Pallas kernels, pack_call(): pl.pallas_call(pack_kernel, out_shape=(jax.ShapeDtypeStruct((OWN, 8, BLK)...  3.24 us
  transfers between devices with their start and end apart: 3, of which 2 were waited for; matrix products, arithmetic and copies ran while one was open for 1% of the time, Pallas kernels for 27%

profile of v4, /device:TPU:4, one launch (start us, length us, event | category | flops | bytes accessed | tf_op | source)
XLA Modules:
  0.0 70.6 jit_solution(14161414929203832283)
XLA Ops:
  0.0 3.2 %pack.1 = (f32[24,8,128]{2,1,0:T(8,128)}, bf16[96,4992]{1,0:T(8,128)(2,1)}, bf16[96,4992]{1,0:T(8,128)(2,1)}) custom-call(bf16[96,9216]{1,0:T(8,128)(2,1)} %panel.1, f32[3,3072]{1,0:T(4,128)} %positions_hbm.1, s32[24,128]{1,0:T(8,128)} %bitcast.4, f32[1,5]{1,0:T(1,128)} %bitcast.6, s32[5,24]{1,0:T(8,128)} %bitcast.5), custom_call_target="tpu_custom_call" | custom-call | tf_op jit(solution)/shard_map/pack/pallas_call | solution.py:358
  3.2 3.8 %collective-permute-start = (bf16[96,4992]{1,0:T(8,128)(2,1)}, bf16[96,4992]{1,0:T(8,128)(2,1)S(1)}, u32[]{:S(2)}, u32[]{:S(2)}) collective-permute-start(bf16[96,4992]{1,0:T(8,128)(2,1)} %get-tuple-element.15), channel_id=1, source_target_pairs={{0,16},{16,32},{32,48},{48,64},{64,80},{80,96},{96,112},{112,128},... | collective-permute-start | bytes 2875400 | tf_op jit(solution)/shard_map/ppermute | solution.py:384
  7.1 5.8 %collective-permute-start.1 = (bf16[96,4992]{1,0:T(8,128)(2,1)}, bf16[96,4992]{1,0:T(8,128)(2,1)S(1)}, u32[]{:S(2)}, u32[]{:S(2)}) collective-permute-start(bf16[96,4992]{1,0:T(8,128)(2,1)} %get-tuple-element.16), channel_id=1, source_target_pairs={{16,0},{32,16},{48,32},{64,48},{80,64},{96,80},{112,96},{128,112},... | collective-permute-start | bytes 2875400 | tf_op jit(solution)/shard_map/ppermute | solution.py:385
  12.9 0.7 rsqrt_multiply_fusion
  13.6 0.1 broadcast_in_dim.10.gain
  13.6 0.0 copy-start
  13.6 1.5 %copy-done = bf16[96,9216]{1,0:T(8,128)(2,1)S(1)} copy-done((bf16[96,9216]{1,0:T(8,128)(2,1)S(1)}, bf16[96,9216]{1,0:T(8,128)(2,1)}, u32[]{:S(2)}) %copy-start) | copy-done | bytes 1769496
  15.1 0.0 copy-start.1
  15.1 0.9 %copy-done.1 = f32[24,8,128]{2,1,0:T(8,128)S(1)} copy-done((f32[24,8,128]{2,1,0:T(8,128)S(1)}, f32[24,8,128]{2,1,0:T(8,128)}, u32[]{:S(2)}) %copy-start.1) | copy-done | bytes 98328
  16.0 13.0 %own_pairs.1 = (f32[24,3,8,128]{3,2,1,0:T(8,128)S(1)}, bf16[24,3,128,192]{3,2,1,0:T(8,128)(2,1)S(1)}, f32[24,4,128,128]{3,2,1,0:T(8,128)S(1)}) custom-call(s32[1]{0:T(128)} %bitcast.row, bf16[96,9216]{1,0:T(8,128)(2,1)S(1)} %copy-done, f32[24,8,128]{2,1,0:T(8,128)S(1)} %copy-done.1, f32[96,128]{1,0:T(8,128)S(1)} %broadcast_in_dim.10.gain), custom_call_target="tpu_custom_call" | custom-call | flops 1509949440 | bytes 8388608 | tf_op jit(solution)/shard_map/own_pairs/pallas_call | solution.py:302
  29.0 3.4 %collective-permute-done.message = bf16[96,4992]{1,0:T(8,128)(2,1)S(1)} collective-permute-done((bf16[96,4992]{1,0:T(8,128)(2,1)}, bf16[96,4992]{1,0:T(8,128)(2,1)S(1)}, u32[]{:S(2)}, u32[]{:S(2)}) %collective-permute-start) | collective-permute-done | bytes 958496 | tf_op jit(solution)/shard_map/ppermute | solution.py:384
  32.4 6.1 %below_pairs.1.start = f32[49,3,8,128]{3,2,1,0:T(8,128)S(1)} custom-call(s32[1]{0:T(128)} %bitcast.row, f32[24,3,8,128]{3,2,1,0:T(8,128)S(1)} %get-tuple-element.12.start, bf16[24,3,128,192]{3,2,1,0:T(8,128)(2,1)S(1)} %get-tuple-element.13.scaled, f32[24,4,128,128]{3,2,1,0:T(8,128)S(1)} %get-tuple-element.14.geo_col, ...), custom_call_target="tpu_custom_call" | custom-call | flops 1132462080 | bytes 8388608 | tf_op jit(solution)/shard_map/below_pairs/pallas_call | solution.py:333
  38.5 0.0 collective-permute-done.1.message
  38.5 9.7 %above_pairs.1 = f32[16,6,192]{2,1,0:T(8,128)S(1)} custom-call(s32[1]{0:T(128)} %bitcast.row, f32[49,3,8,128]{3,2,1,0:T(8,128)S(1)} %below_pairs.1.start, bf16[24,3,128,192]{3,2,1,0:T(8,128)(2,1)S(1)} %get-tuple-element.13.scaled, f32[24,4,128,128]{3,2,1,0:T(8,128)S(1)} %get-tuple-element.14.geo_col, bf16[96,4992]{1,0:T(8,128)(2,1)S(1)} %collective-permute-done.1.message, ...), custom_call_target="tpu_custom_call" | custom-call | flops 1132462080 | bytes 8388608 | tf_op jit(solution)/shard_map/above_pairs/pallas_call | solution.py:333
  48.3 12.6 %all_to_all.5 = f32[16,6,192]{2,1,0:T(8,128)S(1)} all-to-all(f32[16,6,192]{2,1,0:T(8,128)S(1)} %above_pairs.1), channel_id=1, replica_groups=mesh['row'=16,'col'=16] {'col'}, dimensions={0} | all-to-all | bytes 147456 | tf_op jit(solution)/shard_map/all_to_all | solution.py:394
  60.9 1.9 %collective-permute-start.2 = (f32[3,192]{1,0:T(4,128)S(1)}, f32[3,192]{1,0:T(4,128)S(1)}, u32[]{:S(2)}, u32[]{:S(2)}) collective-permute-start(f32[3,192]{1,0:T(4,128)S(1)} %slice.9), channel_id=1, source_target_pairs={{0,16},{1,17},{2,18},{3,19},{4,20},{5,21},{6,22},{7,23},{16,32},{1... | collective-permute-start | bytes 6920 | tf_op jit(solution)/shard_map/ppermute | solution.py:401
  62.8 7.2 %collective-permute-done.2 = f32[3,192]{1,0:T(4,128)S(1)} collective-permute-done((f32[3,192]{1,0:T(4,128)S(1)}, f32[3,192]{1,0:T(4,128)S(1)}, u32[]{:S(2)}, u32[]{:S(2)}) %collective-permute-start.2) | collective-permute-done | bytes 2336 | tf_op jit(solution)/shard_map/ppermute | solution.py:401
  70.0 0.6 slice_add_fusion
  (2 shorter events, 0.0 us)
Async XLA Ops:
  3.2 29.1 %collective-permute-start = (bf16[96,4992]{1,0:T(8,128)(2,1)}, bf16[96,4992]{1,0:T(8,128)(2,1)S(1)}, u32[]{:S(2)}, u32[]{:S(2)}) collective-permute-start(bf16[96,4992]{1,0:T(8,128)(2,1)} %get-tuple-element.15), channel_id=1, source_target_pairs={{0,16},{16,32},{32,48},{48,64},{64,80},{80,96},{96,112},{112,128},... | collective-permute-start | bytes 2875400 | tf_op jit(solution)/shard_map/ppermute | solution.py:384
  7.1 31.4 %collective-permute-start.1 = (bf16[96,4992]{1,0:T(8,128)(2,1)}, bf16[96,4992]{1,0:T(8,128)(2,1)S(1)}, u32[]{:S(2)}, u32[]{:S(2)}) collective-permute-start(bf16[96,4992]{1,0:T(8,128)(2,1)} %get-tuple-element.16), channel_id=1, source_target_pairs={{16,0},{32,16},{48,32},{64,48},{80,64},{96,80},{112,96},{128,112},... | collective-permute-start | bytes 2875400 | tf_op jit(solution)/shard_map/ppermute | solution.py:385
  13.6 1.5 %copy-start = (bf16[96,9216]{1,0:T(8,128)(2,1)S(1)}, bf16[96,9216]{1,0:T(8,128)(2,1)}, u32[]{:S(2)}) copy-start(bf16[96,9216]{1,0:T(8,128)(2,1)} %panel.1) | copy-start | bytes 5308420
  15.1 0.9 %copy-start.1 = (f32[24,8,128]{2,1,0:T(8,128)S(1)}, f32[24,8,128]{2,1,0:T(8,128)}, u32[]{:S(2)}) copy-start(f32[24,8,128]{2,1,0:T(8,128)} %get-tuple-element.11.geo) | copy-start | bytes 294916
  60.9 9.1 %collective-permute-start.2 = (f32[3,192]{1,0:T(4,128)S(1)}, f32[3,192]{1,0:T(4,128)S(1)}, u32[]{:S(2)}, u32[]{:S(2)}) collective-permute-start(f32[3,192]{1,0:T(4,128)S(1)} %slice.9), channel_id=1, source_target_pairs={{0,16},{1,17},{2,18},{3,19},{4,20},{5,21},{6,22},{7,23},{16,32},{1... | collective-permute-start | bytes 6920 | tf_op jit(solution)/shard_map/ppermute | solution.py:401
